TPU v7x, 512 devices: a whole 4x4x16 slice. The times are simulated.
512 devices in a mesh: blk: 32 (over x, z_lo), uly: 4 (over y), tp: 4 (over z_hi, core).
Axes of the slice: x: 4, y: 4, z: 16 (z_hi: 2, z_lo: 8; z = z_hi * 8 + z_lo), core: 2. Of those that a mesh axis runs over, the one named last changes fastest.
Arguments:
- query_matrix: bfloat16 [8192, 4, 768], P(('blk', 'uly'), None, 'tp'), may hold values from -16 to 16
- key_matrix: bfloat16 [8192, 384], P(('blk', 'uly')), may hold values from -8 to 8
- value_matrix: bfloat16 [8192, 384], P(('blk', 'uly')), may hold values from -6 to 6
- output_gradient: bfloat16 [8192, 4, 768], P(('blk', 'uly'), None, 'tp'), may hold values from -16 to 16
- stripe_map: int32 [128], replicated, may hold values from 0 to 127, each once
Outputs:
- query_gradients: bfloat16 [8192, 4, 768], P(('blk', 'uly'), None, 'tp')
- key_gradients: bfloat16 [8192, 384], P(('blk', 'uly'), 'tp')
- value_gradients: bfloat16 [8192, 384], P(('blk', 'uly'), 'tp')
Inputs may be any that keep to these rules, and one draw needn't show every extreme that they name: `stripe_map`: each of the 128 sequence blocks is held by exactly one stored block.
All inputs are finite; a program needn't handle non-finite values.
Results may differ from a plain program's by a relative error of at most 0.025.
Values may be sent and summed in bfloat16 or wider, within the bound.
A program may use at most 64 MiB of HBM per device.

v0:
```python
import jax
import jax.numpy as jnp
from jax import lax
from jax.sharding import PartitionSpec as P

HEAD_WIDTH = 96


def shifted(value, axis, steps):
    count = lax.axis_size(axis)
    pairs = [(source, (source + steps) % count) for source in range(count)]
    return lax.ppermute(value, axis, pairs)


def per_device(query_matrix, key_matrix, value_matrix, output_gradient, stripe_map):
    cycle_size = lax.axis_size("blk")
    head_split = lax.axis_size("uly")
    tok_count = query_matrix.shape[0]
    score_scale = HEAD_WIDTH ** (-0.5)
    query_post, grad_post, key_post, value_post = (
        lax.all_to_all(query_matrix, "uly", split_axis=1, concat_axis=0, tiled=True),
        lax.all_to_all(output_gradient, "uly", split_axis=1, concat_axis=0, tiled=True),
        lax.all_to_all(key_matrix, "uly", split_axis=1, concat_axis=0, tiled=True),
        lax.all_to_all(value_matrix, "uly", split_axis=1, concat_axis=0, tiled=True),
    )
    row_count = query_post.shape[0]
    group_heads = query_post.shape[1]
    member_heads = query_post.shape[2] // HEAD_WIDTH
    query_heads = query_post.reshape(row_count, group_heads, member_heads, HEAD_WIDTH)
    grad_heads = grad_post.reshape(row_count, group_heads, member_heads, HEAD_WIDTH)
    cycle_rank = lax.axis_index("blk")
    offsets = jnp.arange(tok_count, dtype=jnp.int32)

    def positions(owner):
        blocks = lax.dynamic_slice_in_dim(stripe_map, owner * head_split, head_split)
        return (blocks[:, None] * tok_count + offsets[None, :]).reshape(row_count)

    query_pos = positions(cycle_rank)

    def apply_tile(compute, current):
        return compute(0, row_count, 0, row_count, current)

    def tile_scores(held_keys, key_pos, row_lo, row_hi, col_lo, col_hi):
        key_heads = held_keys.reshape(row_count, group_heads, HEAD_WIDTH)
        scores = (
            jnp.einsum("rgmd,cgd->gmrc", query_heads, key_heads, preferred_element_type=jnp.float32)
            * score_scale
        )
        visible = key_pos[None, col_lo:col_hi] <= query_pos[row_lo:row_hi, None]
        return (scores, visible, key_heads)

    def forward_tile(running, held_pair, key_pos):

        def compute(row_lo, row_hi, col_lo, col_hi, current):
            row_max, row_total, weighted = current
            scores, visible, key_heads = tile_scores(
                held_pair[0], key_pos, row_lo, row_hi, col_lo, col_hi
            )
            value_heads = held_pair[1].reshape(row_count, group_heads, HEAD_WIDTH)
            scores = jnp.where(visible, scores, -jnp.inf)
            old_max = row_max
            new_max = jnp.maximum(old_max, jnp.max(scores, axis=-1))
            rescale = jnp.exp(old_max - new_max)
            weights = jnp.exp(scores - new_max[..., None])
            weights_upper = weights.astype(jnp.bfloat16)
            weights_rest = (weights - weights_upper.astype(jnp.float32)).astype(jnp.bfloat16)
            product = jnp.einsum(
                "gmrc,cgd->gmrd", weights_upper, value_heads, preferred_element_type=jnp.float32
            )
            product = product + jnp.einsum(
                "gmrc,cgd->gmrd", weights_rest, value_heads, preferred_element_type=jnp.float32
            )
            part_total = row_total * rescale + jnp.sum(weights, axis=-1)
            part_weighted = weighted * rescale[..., None] + product
            row_max = row_max.at[..., row_lo:row_hi].set(new_max)
            row_total = row_total.at[..., row_lo:row_hi].set(part_total)
            weighted = weighted.at[..., row_lo:row_hi, :].set(part_weighted)
            return (row_max, row_total, weighted)

        return apply_tile(compute, running)

    def send_keys(held_pair):
        return shifted((held_pair[0], held_pair[1]), "blk", 1)

    def send_grads(partials):
        return shifted((partials[0], partials[1]), "blk", 1)

    kept_blocks = ()

    def forward_turn(cycle_step, carried):
        running, held_pair, stored = carried
        running = forward_tile(
            running, held_pair, positions((cycle_rank - cycle_step) % cycle_size)
        )
        return (running, send_keys(held_pair), stored)

    initial = (
        jnp.full((group_heads, member_heads, row_count), -jnp.inf, jnp.float32),
        jnp.zeros((group_heads, member_heads, row_count), jnp.float32),
        jnp.zeros((group_heads, member_heads, row_count, HEAD_WIDTH), jnp.float32),
    )
    running, held_pair, kept_blocks = lax.fori_loop(
        0, cycle_size - 1, forward_turn, (initial, (key_post, value_post), kept_blocks)
    )
    final_step = cycle_size - 1
    row_max, row_total, weighted = forward_tile(
        running, held_pair, positions((cycle_rank - final_step) % cycle_size)
    )
    log_total = row_max + jnp.log(row_total)
    output_rows = weighted / row_total[..., None]
    output_dot = jnp.sum(
        jnp.transpose(grad_heads, (1, 2, 0, 3)).astype(jnp.float32) * output_rows, axis=-1
    )

    def backward_tile(totals, held_pair, key_pos):

        def compute(row_lo, row_hi, col_lo, col_hi, current):
            query_gradient_part, key_gradient_part, value_gradient_part = current
            scores, visible, key_heads = tile_scores(
                held_pair[0], key_pos, row_lo, row_hi, col_lo, col_hi
            )
            value_heads = held_pair[1].reshape(row_count, group_heads, HEAD_WIDTH)
            probability = jnp.where(
                visible, jnp.exp(scores - log_total[..., row_lo:row_hi, None]), 0.0
            )
            value_gradient_part = value_gradient_part.at[col_lo:col_hi].add(
                jnp.einsum(
                    "gmrc,rgmd->cgd",
                    probability.astype(jnp.bfloat16),
                    grad_heads,
                    preferred_element_type=jnp.float32,
                )
            )
            prob_grads = jnp.einsum(
                "rgmd,cgd->gmrc", grad_heads, value_heads, preferred_element_type=jnp.float32
            )
            score_grads = (
                probability * (prob_grads - output_dot[..., row_lo:row_hi, None])
            ).astype(jnp.bfloat16)
            query_gradient_part = query_gradient_part.at[row_lo:row_hi].add(
                jnp.einsum(
                    "gmrc,cgd->rgmd", score_grads, key_heads, preferred_element_type=jnp.float32
                )
                * score_scale
            )
            key_gradient_part = key_gradient_part.at[col_lo:col_hi].add(
                jnp.einsum(
                    "gmrc,rgmd->cgd", score_grads, query_heads, preferred_element_type=jnp.float32
                )
                * score_scale
            )
            return (query_gradient_part, key_gradient_part, value_gradient_part)

        return apply_tile(compute, totals)

    zero_query = jnp.zeros((row_count, group_heads, member_heads, HEAD_WIDTH), jnp.float32)
    zero_pair = jnp.zeros((row_count, group_heads, HEAD_WIDTH), jnp.float32)

    def passed_turn(cycle_step, carried):
        totals, held_now = carried
        query_gradient_part, key_gradient_part, value_gradient_part = backward_tile(
            totals, held_now, positions((cycle_rank - cycle_step) % cycle_size)
        )
        key_gradient_part, value_gradient_part = send_grads(
            (key_gradient_part, value_gradient_part)
        )
        return ((query_gradient_part, key_gradient_part, value_gradient_part), send_keys(held_now))

    totals, held_now = lax.fori_loop(
        0, cycle_size - 1, passed_turn, ((zero_query, zero_pair, zero_pair), (key_post, value_post))
    )
    query_gradient_part, key_gradient_part, value_gradient_part = backward_tile(
        totals, held_now, positions((cycle_rank - final_step) % cycle_size)
    )
    key_gradient_part, value_gradient_part = send_grads((key_gradient_part, value_gradient_part))
    query_out = query_gradient_part.reshape(row_count, group_heads, member_heads * HEAD_WIDTH)
    key_out = key_gradient_part.reshape(row_count, group_heads * HEAD_WIDTH)
    value_out = value_gradient_part.reshape(row_count, group_heads * HEAD_WIDTH)
    query_back, key_back, value_back = (
        lax.all_to_all(query_out, "uly", split_axis=0, concat_axis=1, tiled=True),
        lax.all_to_all(key_out, "uly", split_axis=0, concat_axis=1, tiled=True),
        lax.all_to_all(value_out, "uly", split_axis=0, concat_axis=1, tiled=True),
    )
    key_sum, value_sum = (
        lax.psum_scatter(key_back, "tp", scatter_dimension=1, tiled=True),
        lax.psum_scatter(value_back, "tp", scatter_dimension=1, tiled=True),
    )
    return (
        query_back.astype(jnp.bfloat16),
        key_sum.astype(jnp.bfloat16),
        value_sum.astype(jnp.bfloat16),
    )


def solution(mesh):
    return jax.shard_map(
        per_device,
        mesh=mesh,
        in_specs=(
            P(("blk", "uly"), None, "tp"),
            P(("blk", "uly"), None),
            P(("blk", "uly"), None),
            P(("blk", "uly"), None, "tp"),
            P(),
        ),
        out_specs=(P(("blk", "uly"), None, "tp"), P(("blk", "uly"), "tp"), P(("blk", "uly"), "tp")),
        check_vma=False,
    )
```

profile of v0, /device:TPU:1, one launch (start us, length us, event | category | flops | bytes accessed | tf_op | source)
XLA Modules:
  0.0 1404.8 jit_solution(9767353934797185522)
XLA Ops:
  44.1 484.3 %while.114 = (s32[]{:T(128)}, f32[1,2,256]{2,1,0:T(2,128)S(1)}, f32[1,2,256]{2,1,0:T(2,128)S(1)}, f32[1,2,256,96]{2,3,1,0:T(8,128)S(1)}, bf16[256,96]{0,1:T(8,12...) while((s32[]{:T(128)}, f32[1,2,256]{2,1,0:T(2,128)S(1)}, ...), condition=%wide.region_3.4_spmd.clone, body=%wide.region_0.3_spmd.clone.sunk | while | flops 77336592 | bytes 3891676 | solution.py:102
  67.4 8.2 collective-permute-done.1
  82.9 8.2 collective-permute-done.1
  98.4 8.2 collective-permute-done.1
  113.8 8.2 collective-permute-done.1
  144.8 8.8 collective-permute-done.1
  160.3 8.2 collective-permute-done.1
  175.8 8.3 collective-permute-done.1
  191.3 8.3 collective-permute-done.1
  207.1 8.2 collective-permute-done.1
  222.6 8.3 collective-permute-done.1
  238.1 8.2 collective-permute-done.1
  269.0 8.2 collective-permute-done.1
  284.5 8.2 collective-permute-done.1
  300.0 8.2 collective-permute-done.1
  315.5 8.2 collective-permute-done.1
  331.0 8.2 collective-permute-done.1
  346.4 8.3 collective-permute-done.1
  361.9 8.2 collective-permute-done.1
  377.4 8.6 collective-permute-done.1
  392.9 8.5 collective-permute-done.1
  408.7 8.2 collective-permute-done.1
  440.4 8.2 collective-permute-done.1
  471.8 8.2 collective-permute-done.1
  487.3 8.2 collective-permute-done.1
  502.8 8.2 collective-permute-done.1
  518.2 8.2 collective-permute-done.1
  530.4 695.1 %while.115 = (s32[]{:T(128)}, f32[256,1,2,96]{0,3,2,1:T(8,128)S(1)}, f32[256,1,96]{0,2,1:T(8,128)S(1)}, f32[256,1,96]{0,2,1:T(8,128)S(1)}, bf16[256,96]{0,1:T(8,...) while((s32[]{:T(128)}, f32[256,1,2,96]{0,3,2,1:T(8,128)S(1)}, ...), condition=%wide.region_8.9_spmd.clone, body=%wide.region_7.8_spmd.clone.sunk | while | flops 127033872 | bytes 5206594 | solution.py:169
  1227.9 12.1 collective-permute-done.7
  1252.1 12.4 collective-permute-done.6
  1282.4 66.9 %reduce-scatter.9.cloned.1.call-done = f32[96,64]{1,0:T(8,128)} async-done(((f32[384,64]{1,0:T(8,128)}), f32[96,64]{1,0:T(8,128)}) %reduce-scatter.9.cloned.1.call-update) | async-done | bytes 24592
  1350.7 45.8 %reduce-scatter.7.cloned.1.call-done = f32[96,64]{1,0:T(8,128)} async-done(((f32[384,64]{1,0:T(8,128)}), f32[96,64]{1,0:T(8,128)}) %reduce-scatter.7.cloned.1.call-update) | async-done | bytes 24592
  (1272 shorter events, 1031.0 us)
Async XLA Ops:
  44.1 16.0 %collective-permute-start.1 = (bf16[256,96]{0,1:T(8,128)(2,1)S(1)}, bf16[256,96]{0,1:T(8,128)(2,1)S(1)}, u32[]{:S(2)}, u32[]{:S(2)}) collective-permute-start(bf16[256,96]{0,1:T(8,128)(2,1)S(1)} %copy.160), channel_id=1, source_target_pairs={{0,16},{16,32},{32,48},{48,64},{64,80},{80,96},{96,112},{112,128},... | collective-permute-start | bytes 147464 | tf_op jit(solution)/shard_map/while/body/eval_jaxpr/ppermute | solution.py:12
  47.2 14.9 %collective-permute-start = (bf16[256,96]{0,1:T(8,128)(2,1)S(1)}, bf16[256,96]{0,1:T(8,128)(2,1)S(1)}, u32[]{:S(2)}, u32[]{:S(2)}) collective-permute-start(bf16[256,96]{0,1:T(8,128)(2,1)S(1)} %copy.159), channel_id=1, source_target_pairs={{0,16},{16,32},{32,48},{48,64},{64,80},{80,96},{96,112},{112,128},... | collective-permute-start | bytes 147464 | tf_op jit(solution)/shard_map/while/body/eval_jaxpr/ppermute | solution.py:12
  600.1 15.1 %collective-permute-start.2 = (f32[256,1,96]{0,2,1:T(8,128)S(1)}, f32[256,1,96]{0,2,1:T(8,128)S(1)}, u32[]{:S(2)}, u32[]{:S(2)}) collective-permute-start(f32[256,1,96]{0,2,1:T(8,128)S(1)} %fusion.147), channel_id=1, source_target_pairs={{0,16},{16,32},{32,48},{48,64},{64,80},{80,96},{96,112},{112,128},... | collective-permute-start | bytes 294920 | tf_op jit(solution)/shard_map/while/body/eval_jaxpr/ppermute | solution.py:12
  602.3 15.1 %collective-permute-start.3 = (f32[256,1,96]{0,2,1:T(8,128)S(1)}, f32[256,1,96]{0,2,1:T(8,128)S(1)}, u32[]{:S(2)}, u32[]{:S(2)}) collective-permute-start(f32[256,1,96]{0,2,1:T(8,128)S(1)} %fusion.148), channel_id=1, source_target_pairs={{0,16},{16,32},{32,48},{48,64},{64,80},{80,96},{96,112},{112,128},... | collective-permute-start | bytes 294920 | tf_op jit(solution)/shard_map/while/body/eval_jaxpr/ppermute | solution.py:12
  646.2 15.3 %collective-permute-start.3 = (f32[256,1,96]{0,2,1:T(8,128)S(1)}, f32[256,1,96]{0,2,1:T(8,128)S(1)}, u32[]{:S(2)}, u32[]{:S(2)}) collective-permute-start(f32[256,1,96]{0,2,1:T(8,128)S(1)} %fusion.148), channel_id=1, source_target_pairs={{0,16},{16,32},{32,48},{48,64},{64,80},{80,96},{96,112},{112,128},... | collective-permute-start | bytes 294920 | tf_op jit(solution)/shard_map/while/body/eval_jaxpr/ppermute | solution.py:12
  668.8 15.4 %collective-permute-start.3 = (f32[256,1,96]{0,2,1:T(8,128)S(1)}, f32[256,1,96]{0,2,1:T(8,128)S(1)}, u32[]{:S(2)}, u32[]{:S(2)}) collective-permute-start(f32[256,1,96]{0,2,1:T(8,128)S(1)} %fusion.148), channel_id=1, source_target_pairs={{0,16},{16,32},{32,48},{48,64},{64,80},{80,96},{96,112},{112,128},... | collective-permute-start | bytes 294920 | tf_op jit(solution)/shard_map/while/body/eval_jaxpr/ppermute | solution.py:12
  691.5 15.0 %collective-permute-start.3 = (f32[256,1,96]{0,2,1:T(8,128)S(1)}, f32[256,1,96]{0,2,1:T(8,128)S(1)}, u32[]{:S(2)}, u32[]{:S(2)}) collective-permute-start(f32[256,1,96]{0,2,1:T(8,128)S(1)} %fusion.148), channel_id=1, source_target_pairs={{0,16},{16,32},{32,48},{48,64},{64,80},{80,96},{96,112},{112,128},... | collective-permute-start | bytes 294920 | tf_op jit(solution)/shard_map/while/body/eval_jaxpr/ppermute | solution.py:12
  713.9 15.4 %collective-permute-start.3 = (f32[256,1,96]{0,2,1:T(8,128)S(1)}, f32[256,1,96]{0,2,1:T(8,128)S(1)}, u32[]{:S(2)}, u32[]{:S(2)}) collective-permute-start(f32[256,1,96]{0,2,1:T(8,128)S(1)} %fusion.148), channel_id=1, source_target_pairs={{0,16},{16,32},{32,48},{48,64},{64,80},{80,96},{96,112},{112,128},... | collective-permute-start | bytes 294920 | tf_op jit(solution)/shard_map/while/body/eval_jaxpr/ppermute | solution.py:12
  736.7 15.0 %collective-permute-start.3 = (f32[256,1,96]{0,2,1:T(8,128)S(1)}, f32[256,1,96]{0,2,1:T(8,128)S(1)}, u32[]{:S(2)}, u32[]{:S(2)}) collective-permute-start(f32[256,1,96]{0,2,1:T(8,128)S(1)} %fusion.148), channel_id=1, source_target_pairs={{0,16},{16,32},{32,48},{48,64},{64,80},{80,96},{96,112},{112,128},... | collective-permute-start | bytes 294920 | tf_op jit(solution)/shard_map/while/body/eval_jaxpr/ppermute | solution.py:12
  759.0 15.4 %collective-permute-start.3 = (f32[256,1,96]{0,2,1:T(8,128)S(1)}, f32[256,1,96]{0,2,1:T(8,128)S(1)}, u32[]{:S(2)}, u32[]{:S(2)}) collective-permute-start(f32[256,1,96]{0,2,1:T(8,128)S(1)} %fusion.148), channel_id=1, source_target_pairs={{0,16},{16,32},{32,48},{48,64},{64,80},{80,96},{96,112},{112,128},... | collective-permute-start | bytes 294920 | tf_op jit(solution)/shard_map/while/body/eval_jaxpr/ppermute | solution.py:12
  781.8 15.0 %collective-permute-start.3 = (f32[256,1,96]{0,2,1:T(8,128)S(1)}, f32[256,1,96]{0,2,1:T(8,128)S(1)}, u32[]{:S(2)}, u32[]{:S(2)}) collective-permute-start(f32[256,1,96]{0,2,1:T(8,128)S(1)} %fusion.148), channel_id=1, source_target_pairs={{0,16},{16,32},{32,48},{48,64},{64,80},{80,96},{96,112},{112,128},... | collective-permute-start | bytes 294920 | tf_op jit(solution)/shard_map/while/body/eval_jaxpr/ppermute | solution.py:12
  804.1 15.4 %collective-permute-start.3 = (f32[256,1,96]{0,2,1:T(8,128)S(1)}, f32[256,1,96]{0,2,1:T(8,128)S(1)}, u32[]{:S(2)}, u32[]{:S(2)}) collective-permute-start(f32[256,1,96]{0,2,1:T(8,128)S(1)} %fusion.148), channel_id=1, source_target_pairs={{0,16},{16,32},{32,48},{48,64},{64,80},{80,96},{96,112},{112,128},... | collective-permute-start | bytes 294920 | tf_op jit(solution)/shard_map/while/body/eval_jaxpr/ppermute | solution.py:12
  826.9 15.0 %collective-permute-start.3 = (f32[256,1,96]{0,2,1:T(8,128)S(1)}, f32[256,1,96]{0,2,1:T(8,128)S(1)}, u32[]{:S(2)}, u32[]{:S(2)}) collective-permute-start(f32[256,1,96]{0,2,1:T(8,128)S(1)} %fusion.148), channel_id=1, source_target_pairs={{0,16},{16,32},{32,48},{48,64},{64,80},{80,96},{96,112},{112,128},... | collective-permute-start | bytes 294920 | tf_op jit(solution)/shard_map/while/body/eval_jaxpr/ppermute | solution.py:12
  849.2 15.4 %collective-permute-start.3 = (f32[256,1,96]{0,2,1:T(8,128)S(1)}, f32[256,1,96]{0,2,1:T(8,128)S(1)}, u32[]{:S(2)}, u32[]{:S(2)}) collective-permute-start(f32[256,1,96]{0,2,1:T(8,128)S(1)} %fusion.148), channel_id=1, source_target_pairs={{0,16},{16,32},{32,48},{48,64},{64,80},{80,96},{96,112},{112,128},... | collective-permute-start | bytes 294920 | tf_op jit(solution)/shard_map/while/body/eval_jaxpr/ppermute | solution.py:12
  872.0 15.0 %collective-permute-start.3 = (f32[256,1,96]{0,2,1:T(8,128)S(1)}, f32[256,1,96]{0,2,1:T(8,128)S(1)}, u32[]{:S(2)}, u32[]{:S(2)}) collective-permute-start(f32[256,1,96]{0,2,1:T(8,128)S(1)} %fusion.148), channel_id=1, source_target_pairs={{0,16},{16,32},{32,48},{48,64},{64,80},{80,96},{96,112},{112,128},... | collective-permute-start | bytes 294920 | tf_op jit(solution)/shard_map/while/body/eval_jaxpr/ppermute | solution.py:12
  894.3 15.4 %collective-permute-start.3 = (f32[256,1,96]{0,2,1:T(8,128)S(1)}, f32[256,1,96]{0,2,1:T(8,128)S(1)}, u32[]{:S(2)}, u32[]{:S(2)}) collective-permute-start(f32[256,1,96]{0,2,1:T(8,128)S(1)} %fusion.148), channel_id=1, source_target_pairs={{0,16},{16,32},{32,48},{48,64},{64,80},{80,96},{96,112},{112,128},... | collective-permute-start | bytes 294920 | tf_op jit(solution)/shard_map/while/body/eval_jaxpr/ppermute | solution.py:12
  917.1 15.0 %collective-permute-start.3 = (f32[256,1,96]{0,2,1:T(8,128)S(1)}, f32[256,1,96]{0,2,1:T(8,128)S(1)}, u32[]{:S(2)}, u32[]{:S(2)}) collective-permute-start(f32[256,1,96]{0,2,1:T(8,128)S(1)} %fusion.148), channel_id=1, source_target_pairs={{0,16},{16,32},{32,48},{48,64},{64,80},{80,96},{96,112},{112,128},... | collective-permute-start | bytes 294920 | tf_op jit(solution)/shard_map/while/body/eval_jaxpr/ppermute | solution.py:12
  939.4 15.4 %collective-permute-start.3 = (f32[256,1,96]{0,2,1:T(8,128)S(1)}, f32[256,1,96]{0,2,1:T(8,128)S(1)}, u32[]{:S(2)}, u32[]{:S(2)}) collective-permute-start(f32[256,1,96]{0,2,1:T(8,128)S(1)} %fusion.148), channel_id=1, source_target_pairs={{0,16},{16,32},{32,48},{48,64},{64,80},{80,96},{96,112},{112,128},... | collective-permute-start | bytes 294920 | tf_op jit(solution)/shard_map/while/body/eval_jaxpr/ppermute | solution.py:12
  962.2 15.0 %collective-permute-start.3 = (f32[256,1,96]{0,2,1:T(8,128)S(1)}, f32[256,1,96]{0,2,1:T(8,128)S(1)}, u32[]{:S(2)}, u32[]{:S(2)}) collective-permute-start(f32[256,1,96]{0,2,1:T(8,128)S(1)} %fusion.148), channel_id=1, source_target_pairs={{0,16},{16,32},{32,48},{48,64},{64,80},{80,96},{96,112},{112,128},... | collective-permute-start | bytes 294920 | tf_op jit(solution)/shard_map/while/body/eval_jaxpr/ppermute | solution.py:12
  984.5 15.4 %collective-permute-start.3 = (f32[256,1,96]{0,2,1:T(8,128)S(1)}, f32[256,1,96]{0,2,1:T(8,128)S(1)}, u32[]{:S(2)}, u32[]{:S(2)}) collective-permute-start(f32[256,1,96]{0,2,1:T(8,128)S(1)} %fusion.148), channel_id=1, source_target_pairs={{0,16},{16,32},{32,48},{48,64},{64,80},{80,96},{96,112},{112,128},... | collective-permute-start | bytes 294920 | tf_op jit(solution)/shard_map/while/body/eval_jaxpr/ppermute | solution.py:12
  1007.3 15.0 %collective-permute-start.3 = (f32[256,1,96]{0,2,1:T(8,128)S(1)}, f32[256,1,96]{0,2,1:T(8,128)S(1)}, u32[]{:S(2)}, u32[]{:S(2)}) collective-permute-start(f32[256,1,96]{0,2,1:T(8,128)S(1)} %fusion.148), channel_id=1, source_target_pairs={{0,16},{16,32},{32,48},{48,64},{64,80},{80,96},{96,112},{112,128},... | collective-permute-start | bytes 294920 | tf_op jit(solution)/shard_map/while/body/eval_jaxpr/ppermute | solution.py:12
  1029.6 15.4 %collective-permute-start.3 = (f32[256,1,96]{0,2,1:T(8,128)S(1)}, f32[256,1,96]{0,2,1:T(8,128)S(1)}, u32[]{:S(2)}, u32[]{:S(2)}) collective-permute-start(f32[256,1,96]{0,2,1:T(8,128)S(1)} %fusion.148), channel_id=1, source_target_pairs={{0,16},{16,32},{32,48},{48,64},{64,80},{80,96},{96,112},{112,128},... | collective-permute-start | bytes 294920 | tf_op jit(solution)/shard_map/while/body/eval_jaxpr/ppermute | solution.py:12
  1052.4 15.0 %collective-permute-start.3 = (f32[256,1,96]{0,2,1:T(8,128)S(1)}, f32[256,1,96]{0,2,1:T(8,128)S(1)}, u32[]{:S(2)}, u32[]{:S(2)}) collective-permute-start(f32[256,1,96]{0,2,1:T(8,128)S(1)} %fusion.148), channel_id=1, source_target_pairs={{0,16},{16,32},{32,48},{48,64},{64,80},{80,96},{96,112},{112,128},... | collective-permute-start | bytes 294920 | tf_op jit(solution)/shard_map/while/body/eval_jaxpr/ppermute | solution.py:12
  1074.7 15.4 %collective-permute-start.3 = (f32[256,1,96]{0,2,1:T(8,128)S(1)}, f32[256,1,96]{0,2,1:T(8,128)S(1)}, u32[]{:S(2)}, u32[]{:S(2)}) collective-permute-start(f32[256,1,96]{0,2,1:T(8,128)S(1)} %fusion.148), channel_id=1, source_target_pairs={{0,16},{16,32},{32,48},{48,64},{64,80},{80,96},{96,112},{112,128},... | collective-permute-start | bytes 294920 | tf_op jit(solution)/shard_map/while/body/eval_jaxpr/ppermute | solution.py:12
  1097.5 15.0 %collective-permute-start.3 = (f32[256,1,96]{0,2,1:T(8,128)S(1)}, f32[256,1,96]{0,2,1:T(8,128)S(1)}, u32[]{:S(2)}, u32[]{:S(2)}) collective-permute-start(f32[256,1,96]{0,2,1:T(8,128)S(1)} %fusion.148), channel_id=1, source_target_pairs={{0,16},{16,32},{32,48},{48,64},{64,80},{80,96},{96,112},{112,128},... | collective-permute-start | bytes 294920 | tf_op jit(solution)/shard_map/while/body/eval_jaxpr/ppermute | solution.py:12
  1119.8 15.4 %collective-permute-start.3 = (f32[256,1,96]{0,2,1:T(8,128)S(1)}, f32[256,1,96]{0,2,1:T(8,128)S(1)}, u32[]{:S(2)}, u32[]{:S(2)}) collective-permute-start(f32[256,1,96]{0,2,1:T(8,128)S(1)} %fusion.148), channel_id=1, source_target_pairs={{0,16},{16,32},{32,48},{48,64},{64,80},{80,96},{96,112},{112,128},... | collective-permute-start | bytes 294920 | tf_op jit(solution)/shard_map/while/body/eval_jaxpr/ppermute | solution.py:12
  1142.6 15.0 %collective-permute-start.3 = (f32[256,1,96]{0,2,1:T(8,128)S(1)}, f32[256,1,96]{0,2,1:T(8,128)S(1)}, u32[]{:S(2)}, u32[]{:S(2)}) collective-permute-start(f32[256,1,96]{0,2,1:T(8,128)S(1)} %fusion.148), channel_id=1, source_target_pairs={{0,16},{16,32},{32,48},{48,64},{64,80},{80,96},{96,112},{112,128},... | collective-permute-start | bytes 294920 | tf_op jit(solution)/shard_map/while/body/eval_jaxpr/ppermute | solution.py:12
  1164.9 15.4 %collective-permute-start.3 = (f32[256,1,96]{0,2,1:T(8,128)S(1)}, f32[256,1,96]{0,2,1:T(8,128)S(1)}, u32[]{:S(2)}, u32[]{:S(2)}) collective-permute-start(f32[256,1,96]{0,2,1:T(8,128)S(1)} %fusion.148), channel_id=1, source_target_pairs={{0,16},{16,32},{32,48},{48,64},{64,80},{80,96},{96,112},{112,128},... | collective-permute-start | bytes 294920 | tf_op jit(solution)/shard_map/while/body/eval_jaxpr/ppermute | solution.py:12
  1187.7 15.0 %collective-permute-start.3 = (f32[256,1,96]{0,2,1:T(8,128)S(1)}, f32[256,1,96]{0,2,1:T(8,128)S(1)}, u32[]{:S(2)}, u32[]{:S(2)}) collective-permute-start(f32[256,1,96]{0,2,1:T(8,128)S(1)} %fusion.148), channel_id=1, source_target_pairs={{0,16},{16,32},{32,48},{48,64},{64,80},{80,96},{96,112},{112,128},... | collective-permute-start | bytes 294920 | tf_op jit(solution)/shard_map/while/body/eval_jaxpr/ppermute | solution.py:12
  1210.0 15.4 %collective-permute-start.3 = (f32[256,1,96]{0,2,1:T(8,128)S(1)}, f32[256,1,96]{0,2,1:T(8,128)S(1)}, u32[]{:S(2)}, u32[]{:S(2)}) collective-permute-start(f32[256,1,96]{0,2,1:T(8,128)S(1)} %fusion.148), channel_id=1, source_target_pairs={{0,16},{16,32},{32,48},{48,64},{64,80},{80,96},{96,112},{112,128},... | collective-permute-start | bytes 294920 | tf_op jit(solution)/shard_map/while/body/eval_jaxpr/ppermute | solution.py:12
  1244.1 105.1 %reduce-scatter.9.cloned.1.call-start = ((), (), s32[]{:S(2)}) async-start(), calls=%async_computation.10 | async-start | bytes 245760
  1249.9 146.5 %reduce-scatter.7.cloned.1.call-start = ((), (), s32[]{:S(2)}) async-start(), calls=%async_computation.9 | async-start | bytes 245760
  (173 other events, 2253.5 us)
Sparse Core Ops, SparseCore 0:
  1250.1 99.1 reduce-scatter.8
  1352.2 44.2 reduce-scatter.6
where the time goes:
time: 1410 us; the launch traced here: 1400 us
  waiting for transfers between devices  876 us (62%)
  starting transfers between devices  382 us (27%)
  matrix products  61.2 us (4%)
  local copies, waits for them, and re-layouts  25.7 us (2%)
  other arithmetic  25.4 us (2%)
  between operations  14.4 us (1%)
  blocking collectives  14.2 us (1%)
    ppermute x188, waiting for transfers between devices, shifted(): return lax.ppermute(value, axis, pairs)  743 us
    ppermute x188, starting transfers between devices, shifted(): return lax.ppermute(value, axis, pairs)  363 us
    unnamed x4, waiting for transfers between devices  113 us
  transfers between devices with their start and end apart: 195, of which 195 were waited for; matrix products, arithmetic and copies ran while one was open for 7% of the time, Pallas kernels for 0%

commit v1 on v0

v1 whole, which is shorter than its diff:
```python
import jax
import jax.numpy as jnp
from jax import lax
from jax.experimental import pallas as pl
from jax.experimental.pallas import tpu as pltpu
from jax.sharding import PartitionSpec as P

HEAD = 96
WIDE = 2 * HEAD
TOK = 64
LOG2E = 1.4426950408889634
SCALE = HEAD**-0.5
SCALE2 = SCALE * LOG2E
LOW = -1e30
F32 = jnp.float32
BF16 = jnp.bfloat16
MESH = pl.DeviceIdType.MESH
NT = (((1,), (1,)), ((), ()))
STEPS = (4, 3, -3, 2, -2, 1, -1)
RT = 256


def dot(a, b):
    return jnp.dot(a, b, preferred_element_type=F32)


def kernel(
    stripe, qg, kv, dq_out, dkv_out,
    qga, kva, kvu, kt, wq, wg, prob, grad, stat, stat_in, fac, dqt, dqb, dqr,
    dkf, own, sbs, sbr, l1s, l1r, l2s, l2r,
    loc_sem, kvy_s, kvy_r, qy_s, qy_r, kvz_s, kvz_r, kvs_s, kvs_r, qx_s, qx_r,
    st_s, st_r, sb_s, sb_r, l1_s, l1_r, dq_s, dq_r, l2_s, l2_r,
):
    b, y, t = lax.axis_index("blk"), lax.axis_index("uly"), lax.axis_index("tp")
    x, zl = b // 8, b % 8
    h, c = t // 2, t % 2
    z = h * 8 + zl

    def dev(x_, y_, z_, c_):
        return (x_ * 8 + z_ % 8, y_, (z_ // 8) * 2 + c_)

    def send(src, dst, ss, rs, to):
        copy = pltpu.make_async_remote_copy(
            src_ref=src, dst_ref=dst, send_sem=ss, recv_sem=rs, device_id=to, device_id_type=MESH
        )
        copy.start()
        return copy

    def zstep(k):
        if STEPS[k] == 4:
            return jnp.where(c == 0, 4, 12)
        return STEPS[k] % 16

    barrier = pltpu.get_barrier_semaphore()

    def greet(to):
        pl.semaphore_signal(barrier, inc=1, device_id=to, device_id_type=MESH)

    for i in range(4):
        for j in range(4):
            if i or j:
                greet(dev((x + i) % 4, (y + j) % 4, z, c))
    for d in (-4, -3, -2, -1, 1, 2, 3, 4):
        greet(dev(x, y, (z + d + 16) % 16, c))
    greet(dev(x, y, z, 1 - c))
    mine = (h == y // 2) & (c == y % 2) & (c == y // 2)
    for hs in range(2):
        is_self = mine & (h == hs)

        @pl.when(jnp.logical_not(is_self))
        def _():
            greet(dev(x, t, hs * 8 + zl, y // 2))

    pl.semaphore_wait(barrier, 26 - jnp.where(mine, 1, 0))

    sent = []
    half = pl.ds(pl.multiple_of(16 * c, 16), 16)
    for j in range(1, 4):
        yd = (y + j) % 4
        sent.append(
            send(kv.at[yd, half], kva.at[c, zl, y], kvy_s.at[j], kvy_r.at[j], dev(x, yd, z, c))
        )
    for j in range(1, 4):
        yd = (y + j) % 4
        sent.append(send(qg.at[yd], qga.at[x, y], qy_s.at[j], qy_r.at[j], dev(x, yd, z, c)))
    loc_kv = pltpu.make_async_copy(kv.at[y, half], kva.at[c, zl, y], loc_sem.at[0])
    loc_kv.start()
    loc_qg = pltpu.make_async_copy(qg.at[y], qga.at[x, y], loc_sem.at[1])
    loc_qg.start()
    for i in range(1, 4):
        sent.append(
            send(qg.at[y], qga.at[x, y], qx_s.at[0, i], qx_r.at[i], dev((x + i) % 4, y, z, c))
        )
    loc_kv.wait()
    for j in range(1, 4):
        ys = (y - j + 4) % 4
        pltpu.make_async_copy(kva.at[c, zl, ys], kva.at[c, zl, ys], kvy_r.at[j]).wait()
    for k in range(7):
        sent.append(
            send(
                kva.at[c, zl], kva.at[c, zl], kvz_s.at[k], kvz_r.at[k],
                dev(x, y, (z + zstep(k)) % 16, c),
            )
        )
    sib = dev(x, y, z, 1 - c)
    sent.append(send(kva.at[c, zl], kva.at[c, zl], kvs_s.at[7], kvs_r.at[7], sib))
    for j in range(1, 4):
        ys = (y - j + 4) % 4
        pltpu.make_async_copy(qga.at[x, ys], qga.at[x, ys], qy_r.at[j]).wait()
        for i in range(1, 4):
            sent.append(
                send(
                    qga.at[x, ys], qga.at[x, ys], qx_s.at[j, i], qx_r.at[i],
                    dev((x + i) % 4, y, z, c),
                )
            )
    for k in (5, 6, 3, 4, 1, 2, 0):
        zs = (z - zstep(k) + 16) % 8
        pltpu.make_async_copy(kva.at[c, zs], kva.at[c, zs], kvz_r.at[k]).wait()
        sent.append(send(kva.at[c, zs], kva.at[c, zs], kvs_s.at[k], kvs_r.at[k], sib))
    for k in range(8):
        zs = zl if k == 7 else (z - zstep(k) + 16) % 8
        pltpu.make_async_copy(kva.at[1 - c, zs], kva.at[1 - c, zs], kvs_r.at[k]).wait()

    def unpack(zs, _):
        for ys in range(4):
            for hf in range(2):
                v = kva[hf, zs, ys]
                kvu[zs, TOK * ys + 16 * hf : TOK * ys + 16 * hf + 16, :] = v[:, :WIDE]
                kvu[zs, TOK * ys + 32 + 16 * hf : TOK * ys + 48 + 16 * hf, :] = v[:, WIDE:]
        kt[zs] = jnp.transpose(kvu[zs].astype(F32))[:HEAD].astype(BF16)
        return 0

    lax.fori_loop(0, 8, unpack, 0)

    loc_qg.wait()
    lane = lax.broadcasted_iota(jnp.int32, (1, RT), 1)
    sub = lax.broadcasted_iota(jnp.int32, (TOK, RT), 0)
    low_lanes = lax.broadcasted_iota(jnp.int32, (RT, WIDE), 1) < HEAD

    def rows_pass(xs):
        both = qga[xs].reshape(RT, 2 * WIDE)
        zero = jnp.zeros((RT, WIDE), BF16)
        row_pos = jnp.zeros((1, RT), jnp.int32)
        for ys in range(4):
            first = stripe[(xs * 8 + zl) * 4 + ys] * TOK
            row_pos = jnp.where(lane // TOK == ys, first + lane % TOK, row_pos)
        for m in range(2):
            part = both[:, m * WIDE : (m + 1) * WIDE]
            wq[xs * 2 + m] = jnp.where(low_lanes, part, zero)
            wg[xs * 2 + m] = jnp.where(low_lanes, zero, part)

        def member(m, _):
            rt = xs * 2 + m

            def scores_step(kc, top):
                s = lax.dot_general(kvu[kc], wq[rt], NT, preferred_element_type=F32) * SCALE2
                for ys in range(4):
                    first = stripe[(x * 8 + kc) * 4 + ys] * TOK
                    piece = jnp.where(
                        sub + first <= row_pos, s[TOK * ys : TOK * (ys + 1)], LOW
                    )
                    prob[rt, kc, TOK * ys : TOK * (ys + 1), :] = piece
                    top = jnp.maximum(top, jnp.max(piece.reshape(8, 8, RT), axis=0))
                return top

            top = lax.fori_loop(
                0, 8, scores_step, jnp.full((8, RT), LOW, F32), unroll=8
            )
            top = jnp.max(top, axis=0, keepdims=True)

            def weights_step(kc, sums):
                total, mixed = sums
                pg = lax.dot_general(kvu[kc], wg[rt], NT, preferred_element_type=F32)
                e = jnp.exp2(prob[rt, kc] - top)
                prob[rt, kc] = e
                grad[rt, kc] = pg
                total = total + jnp.sum(e.reshape(32, 8, RT), axis=0)
                mixed = mixed + jnp.sum((e * pg).reshape(32, 8, RT), axis=0)
                return total, mixed

            zero8 = jnp.zeros((8, RT), F32)
            total, mixed = lax.fori_loop(0, 8, weights_step, (zero8, zero8), unroll=8)
            stat[0, pl.ds(rt, 1)] = top
            stat[1, pl.ds(rt, 1)] = jnp.sum(total, axis=0, keepdims=True)
            stat[2, pl.ds(rt, 1)] = jnp.sum(mixed, axis=0, keepdims=True)
            return 0

        lax.fori_loop(0, 2, member, 0)

    rows_pass(x)
    for i in (1, 3, 2):
        xs = (x - i + 4) % 4
        pltpu.make_async_copy(qga.at[xs], qga.at[xs], qx_r.at[i]).wait()
        rows_pass(xs)

    for i in range(1, 4):
        sent.append(
            send(stat, stat_in.at[i], st_s.at[i], st_r.at[i], dev((x + i) % 4, y, z, c))
        )
    dqt[...] = jnp.zeros_like(dqt)
    for i in range(1, 4):
        pltpu.make_async_copy(stat_in.at[i], stat_in.at[i], st_r.at[i]).wait()
    top = stat[0]
    for i in range(1, 4):
        top = jnp.maximum(top, stat_in[i, 0])
    mine_up = jnp.exp2(stat[0] - top)
    total = stat[1] * mine_up
    mixed = stat[2] * mine_up
    for i in range(1, 4):
        up = jnp.exp2(stat_in[i, 0] - top)
        total = total + stat_in[i, 1] * up
        mixed = mixed + stat_in[i, 2] * up
    fac[0] = mine_up / total
    fac[1] = mixed / total

    def give(k):
        pltpu.make_async_copy(sbr.at[k], sbr.at[k], sb_r.at[k]).wait()
        l1s[k] = (own[k] + sbr[k].astype(F32)).astype(BF16)
        sent.append(
            send(
                l1s.at[k], l1r.at[k], l1_s.at[k], l1_r.at[k],
                dev(x, y, (z + zstep(k)) % 16, c),
            )
        )

    for k in range(8):
        kc = zl if k == 7 else (zl + zstep(k)) % 8

        def rows_step(rt, dkv):
            p = prob[rt, kc] * fac[0, pl.ds(rt, 1)]
            ds = (p * (grad[rt, kc] - fac[1, pl.ds(rt, 1)])).astype(BF16)
            dkv = dkv + dot(p.astype(BF16), wg[rt]) + dot(ds, wq[rt])
            dqt[rt] += dot(kt[kc], ds)
            return dkv

        dkf[...] = lax.fori_loop(0, 8, rows_step, jnp.zeros((RT, WIDE), F32), unroll=8)
        sbs[k] = dkf[pl.ds(pl.multiple_of(128 * (1 - c), 128), 128)].astype(BF16)
        own[k] = dkf[pl.ds(pl.multiple_of(128 * c, 128), 128)]
        sent.append(send(sbs.at[k], sbr.at[k], sb_s.at[k], sb_r.at[k], sib))
        if k:
            give(k - 1)

    for i in range(4):
        xs = (x + i) % 4
        pair = dqt[pl.ds(xs * 2, 2)].reshape(WIDE, RT)
        dqb[i] = (jnp.transpose(pair) * SCALE).astype(BF16).reshape(4, TOK, WIDE)
        for j in range(4):
            ys = (y + j) % 4
            if i or j:
                sent.append(
                    send(
                        dqb.at[i, ys], dqr.at[i, y], dq_s.at[i, j], dq_r.at[i, j],
                        dev(xs, ys, z, c),
                    )
                )
            else:
                dqr[0, y] = dqb[0, y]

    pltpu.make_async_copy(sbr.at[7], sbr.at[7], sb_r.at[7]).wait()
    total = own[7] + sbr[7].astype(F32)
    for k in (5, 6, 3, 4, 1, 2, 0):
        pltpu.make_async_copy(l1r.at[k], l1r.at[k], l1_r.at[k]).wait()
        total = total + l1r[k].astype(F32)
    left = lax.broadcasted_iota(jnp.int32, (128, WIDE), 1) < HEAD
    l2s[...] = (total * jnp.where(left, SCALE, 1.0)).astype(BF16).reshape(2, TOK, WIDE)
    for q in range(2):
        yo = 2 * c + q
        is_self = mine & (yo == y)
        to = dev(x, yo, 8 * (y // 2) + zl, y % 2)
        copy = pltpu.make_async_remote_copy(
            src_ref=l2s.at[q], dst_ref=l2r.at[h], send_sem=l2_s.at[q], recv_sem=l2_r.at[h],
            device_id=to, device_id_type=MESH,
        )

        @pl.when(jnp.logical_not(is_self))
        def _():
            copy.start()

        @pl.when(is_self)
        def _():
            l2r[h] = l2s[q]

    for j in range(4):
        gs = (y - j + 4) % 4
        total = jnp.zeros((TOK, WIDE), F32)
        for i in range(4):
            if i or j:
                pltpu.make_async_copy(dqr.at[i, gs], dqr.at[i, gs], dq_r.at[i, j]).wait()
            total = total + dqr[i, gs].astype(F32)
        dq_out[gs] = total.astype(BF16)

    for hs in range(2):
        is_self = mine & (h == hs)

        @pl.when(jnp.logical_not(is_self))
        def _():
            pltpu.make_async_copy(l2r.at[hs], l2r.at[hs], l2_r.at[hs]).wait()

    dkv_out[...] = (l2r[0].astype(F32) + l2r[1].astype(F32)).astype(BF16)
    for copy in sent:
        copy.wait_send()
    for q in range(2):
        is_self = mine & (2 * c + q == y)

        @pl.when(jnp.logical_not(is_self))
        def _():
            pltpu.make_async_copy(l2s.at[q], l2s.at[q], l2_s.at[q]).wait()


def per_device(query_matrix, key_matrix, value_matrix, output_gradient, stripe_map):
    q = query_matrix.reshape(TOK, 4, 2, 1, HEAD)
    g = output_gradient.reshape(TOK, 4, 2, 1, HEAD)
    qg = jnp.concatenate([q, g], axis=3).reshape(TOK, 4, 2 * WIDE).transpose(1, 0, 2)
    k = key_matrix.reshape(2, 32, 4, 1, HEAD)
    v = value_matrix.reshape(2, 32, 4, 1, HEAD)
    kv = jnp.concatenate([k, v], axis=3).transpose(2, 1, 0, 3, 4).reshape(4, 32, 2 * WIDE)
    vmem = pl.BlockSpec(memory_space=pltpu.VMEM)
    dma = pltpu.SemaphoreType.DMA
    dq, dkv = pl.pallas_call(
        kernel,
        out_shape=[
            jax.ShapeDtypeStruct((4, TOK, WIDE), BF16),
            jax.ShapeDtypeStruct((TOK, WIDE), BF16),
        ],
        in_specs=[pl.BlockSpec(memory_space=pltpu.SMEM), vmem, vmem],
        out_specs=[vmem, vmem],
        scratch_shapes=[
            pltpu.VMEM((4, 4, TOK, 2 * WIDE), BF16),
            pltpu.VMEM((2, 8, 4, 16, 2 * WIDE), BF16),
            pltpu.VMEM((8, RT, WIDE), BF16),
            pltpu.VMEM((8, HEAD, RT), BF16),
            pltpu.VMEM((8, RT, WIDE), BF16),
            pltpu.VMEM((8, RT, WIDE), BF16),
            pltpu.VMEM((8, 8, RT, RT), F32),
            pltpu.VMEM((8, 8, RT, RT), F32),
            pltpu.VMEM((3, 8, RT), F32),
            pltpu.VMEM((4, 3, 8, RT), F32),
            pltpu.VMEM((2, 8, RT), F32),
            pltpu.VMEM((8, HEAD, RT), F32),
            pltpu.VMEM((4, 4, TOK, WIDE), BF16),
            pltpu.VMEM((4, 4, TOK, WIDE), BF16),
            pltpu.VMEM((RT, WIDE), F32),
            pltpu.VMEM((8, 128, WIDE), F32),
            pltpu.VMEM((8, 128, WIDE), BF16),
            pltpu.VMEM((8, 128, WIDE), BF16),
            pltpu.VMEM((7, 128, WIDE), BF16),
            pltpu.VMEM((7, 128, WIDE), BF16),
            pltpu.VMEM((2, TOK, WIDE), BF16),
            pltpu.VMEM((2, TOK, WIDE), BF16),
            dma((2,)),
            dma((4,)), dma((4,)), dma((4,)), dma((4,)),
            dma((7,)), dma((7,)), dma((8,)), dma((8,)),
            dma((4, 4)), dma((4,)),
            dma((4,)), dma((4,)), dma((8,)), dma((8,)), dma((7,)), dma((7,)),
            dma((4, 4)), dma((4, 4)), dma((2,)), dma((2,)),
        ],
        compiler_params=pltpu.CompilerParams(
            collective_id=0, has_side_effects=True, vmem_limit_bytes=60 * 2**20
        ),
    )(stripe_map, qg, kv)
    return dq.transpose(1, 0, 2), dkv[:, :HEAD], dkv[:, HEAD:]


def solution(mesh):
    return jax.shard_map(
        per_device,
        mesh=mesh,
        in_specs=(
            P(("blk", "uly"), None, "tp"),
            P(("blk", "uly"), None),
            P(("blk", "uly"), None),
            P(("blk", "uly"), None, "tp"),
            P(),
        ),
        out_specs=(P(("blk", "uly"), None, "tp"), P(("blk", "uly"), "tp"), P(("blk", "uly"), "tp")),
        check_vma=False,
    )
```

time: 1410 us -> 83.8 us (0.06)
  waiting for transfers between devices: 876 us -> 0 us
  starting transfers between devices: 382 us -> 0 us
  Pallas kernels: 0 us -> 73.5 us
  matrix products: 61.2 us -> 0 us
  other arithmetic: 25.4 us -> 1.05 us
  local copies, waits for them, and re-layouts: 25.7 us -> 8.22 us
  blocking collectives: 14.2 us -> 0 us
    ppermute x188 -> x0, waiting for transfers between devices: 743 us -> none  [shifted(): return lax.ppermute(value, axis, pairs)]
    ppermute x188 -> x0, starting transfers between devices: 363 us -> none  [shifted(): return lax.ppermute(value, axis, pairs)]
    unnamed x4 -> x0, waiting for transfers between devices: 113 us -> none
    pallas_call x0 -> x1, Pallas kernels: none -> 73.5 us  [per_device(): pl.pallas_call(kernel, out_shape=[jax.ShapeDtypeStruct((4, TOK, WIDE), BF...]
    dot_general x256 -> x0, matrix products: 61.2 us -> none  [the longest x64 17.5 us: tile_scores(): jnp.einsum('rgmd,cgd->gmrc', query_heads, key_heads, preferred_element_ty...]
    all_to_all x5 -> x0, waiting for transfers between devices: 19.4 us -> none  [the longest x1 4.67 us: per_device(): lax.all_to_all(value_out, 'uly', split_axis=0, concat_axis=1, tiled=True)]
    all_to_all x5 -> x0, starting transfers between devices: 18.5 us -> none  [the longest x1 5.14 us: per_device(): lax.all_to_all(key_matrix, 'uly', split_axis=1, concat_axis=0, tiled=True)]
    all_to_all x2 -> x0, blocking collectives: 14.2 us -> none  [the longest x1 7.21 us: per_device(): lax.all_to_all(key_out, 'uly', split_axis=0, concat_axis=1, tiled=True)]
  transfers between devices with their start and end apart: 195 -> 0, of which waited for: 195 -> 0; matrix products, arithmetic and copies ran while one was open for 7% -> 0% of each run, Pallas kernels for 0% -> 0%
where the time goes in v1:
time: 83.8 us; the launch traced here: 83.5 us
  Pallas kernels  73.5 us (88%)
  local copies, waits for them, and re-layouts  8.22 us (10%)
  other arithmetic  1.05 us (1%)
    pallas_call x1, Pallas kernels, per_device(): pl.pallas_call(kernel, out_shape=[jax.ShapeDtypeStruct((4, TOK, WIDE), BF...  73.5 us
    unnamed x7, local copies, waits for them, and re-layouts  2.97 us

profile of v1, /device:TPU:1, one launch (start us, length us, event | category | flops | bytes accessed | tf_op | source)
XLA Modules:
  0.0 83.5 jit_solution(15980219090275511315)
XLA Ops:
  0.6 1.1 %reshape.24 = bf16[64,4,2,1,96]{4,2,1,0,3:T(2,128)(2,1)S(1)} reshape(bf16[64,4,192]{2,1,0:T(4,128)(2,1)} %param.5) | data formatting | bytes 196608 | tf_op jit(solution)/shard_map/reshape | solution.py:312
  1.7 0.0 copy-start
  1.7 0.3 copy.8
  2.0 0.6 copy-done
  2.6 0.1 reshape.25
  2.7 0.3 copy.9
  3.0 0.7 pad_maximum_fusion
  3.7 0.0 copy-start.1
  3.7 0.9 %reshape.26 = bf16[64,4,384]{2,0,1:T(8,128)(2,1)} reshape(bf16[64,4,2,2,96]{4,3,2,0,1:T(2,128)(2,1)S(1)} %pad_maximum_fusion) | data formatting | bytes 393216 | tf_op jit(solution)/shard_map/reshape | solution.py:314
  4.6 0.0 copy-done.1
  4.6 0.1 reshape.27
  4.7 0.0 copy-start.2
  4.7 0.1 copy.10
  4.8 0.7 copy-done.2
  5.5 0.1 reshape.28
  5.6 0.1 copy.11
  5.7 0.4 maximum_bitcast_fusion
  6.1 0.8 reshape.29.kv
  6.9 73.5 %shard_map.76 = (bf16[4,64,192]{2,1,0:T(8,128)(2,1)}, bf16[64,192]{1,0:T(8,128)(2,1)}) custom-call(s32[128]{0:T(128)} %stripe.1, bf16[4,64,384]{2,1,0:T(8,128)(2,1)} %bitcast.6, bf16[4,32,384]{2,1,0:T(8,128)(2,1)} %reshape.29.kv), custom_call_target="tpu_custom_call" | custom-call | tf_op jit(solution)/shard_map/pallas_call | solution.py:320
  80.4 1.5 %fusion = (bf16[64,96]{1,0:T(8,128)(2,1)}, bf16[64,96]{1,0:T(8,128)(2,1)}) fusion(bf16[64,192]{1,0:T(8,128)(2,1)} %get-tuple-element.6), kind=kLoop, calls=%fused_computation.2 | loop fusion | bytes 49152 | tf_op jit(solution)/shard_map/slice | solution.py:362
  81.8 1.7 %copy.12 = bf16[64,4,192]{2,1,0:T(4,128)(2,1)} copy(bf16[64,4,192]{2,0,1:T(8,128)(2,1)} %bitcast.7) | data formatting | bytes 196608
Async XLA Ops:
  1.7 0.9 %copy-start = (bf16[64,4,192]{2,1,0:T(4,128)(2,1)S(1)}, bf16[64,4,192]{2,1,0:T(4,128)(2,1)}, u32[]{:S(2)}) copy-start(bf16[64,4,192]{2,1,0:T(4,128)(2,1)} %param.8) | copy-start | bytes 294916
  3.7 0.9 %copy-start.1 = (bf16[64,384]{1,0:T(8,128)(2,1)S(1)}, bf16[64,384]{1,0:T(8,128)(2,1)}, u32[]{:S(2)}) copy-start(bf16[64,384]{1,0:T(8,128)(2,1)} %param.6) | copy-start | bytes 147460
  4.7 0.8 copy-start.2

commit v2 on v1

v2 whole, which is shorter than its diff:
```python
import jax
import jax.numpy as jnp
from jax import lax
from jax.experimental import pallas as pl
from jax.experimental.pallas import tpu as pltpu
from jax.sharding import PartitionSpec as P

HEAD = 96
WIDE = 2 * HEAD
TOK = 64
RT = 256
LOG2E = 1.4426950408889634
SCALE = HEAD**-0.5
SCALE2 = SCALE * LOG2E
HIDE = -1e30
FLOOR = -1e29
F32 = jnp.float32
BF16 = jnp.bfloat16
MESH = pl.DeviceIdType.MESH
NT = (((1,), (1,)), ((), ()))
N_SEM = 90


def dot(a, b):
    return jnp.dot(a, b, preferred_element_type=F32)


def kernel(
    stripe, q_in, g_in, k_in, v_in, dq_out, dkv_out,
    qg, kv, qga, kva, kvu, kt, wq, wg, prob, grad,
    tile_top, tile_sum, tile_mix, stat, stat_in, fac, delta,
    dqt, dkf, own, sbs, sbr, l1s, relay, fin, q2s, q2r, q1s, q1r, dqs, l2s, l2r, l2z,
    loc_sem, send_sem, recv_sem, l2_s, l2_r,
):
    b, y, t = lax.axis_index("blk"), lax.axis_index("uly"), lax.axis_index("tp")
    x, zl = b // 8, b % 8
    h, c = t // 2, t % 2
    z = h * 8 + zl

    def dev(x_, y_, z_, c_):
        return (x_ * 8 + z_ % 8, y_, (z_ // 8) * 2 + c_)

    def on_x(i):
        return dev((x + i) % 4, y, z, c)

    def on_y(j):
        return dev(x, (y + j) % 4, z, c)

    def on_z(d):
        return dev(x, y, (z + d) % 16, c)

    sib = dev(x, y, z, 1 - c)
    four = jnp.where(c == 0, 2, 14)
    sent = []
    names = {}

    def send(name, src, dst, to):
        n = names.setdefault(name, len(names))
        copy = pltpu.make_async_remote_copy(
            src_ref=src, dst_ref=dst, send_sem=send_sem.at[n], recv_sem=recv_sem.at[n],
            device_id=to, device_id_type=MESH,
        )
        copy.start()
        sent.append(copy)

    def got(name, ref):
        pltpu.make_async_copy(ref, ref, recv_sem.at[names[name]]).wait()

    barrier = pltpu.get_barrier_semaphore()
    peers = [dev((x + i) % 4, (y + j) % 4, z, c) for i in range(4) for j in range(4) if i or j]
    peers += [on_z(d) for d in (1, 15, 2, 14, 8)]
    peers += [dev(x, (y + j) % 4, z, 1 - c) for j in range(4)]
    for to in peers:
        pl.semaphore_signal(barrier, inc=1, device_id=to, device_id_type=MESH)

    for g in range(4):
        part = slice(g * HEAD, (g + 1) * HEAD)
        kv[g] = jnp.concatenate(
            [k_in[:32, part], v_in[:32, part], k_in[32:, part], v_in[32:, part]], axis=1
        )
        qs, gs = q_in[g], g_in[g]
        qg[g] = jnp.concatenate(
            [qs[:, :HEAD], gs[:, :HEAD], qs[:, HEAD:], gs[:, HEAD:]], axis=1
        )
    pl.semaphore_wait(barrier, len(peers))

    half = pl.ds(pl.multiple_of(16 * c, 16), 16)
    for j in (1, 3, 2):
        send(f"kvy{j}", kv.at[(y + j) % 4, half], kva.at[c, zl, j], on_y(j))
    for d in (1, 15, 2, 14):
        send(f"a{d}", kv.at[y, half], kva.at[c, zl, 0], on_z(d))
    for i in (1, 3):
        send(f"x{i}_0", qg.at[y], qga.at[x, 0], on_x(i))
    for j in (1, 3, 2):
        send(f"qy{j}", qg.at[(y + j) % 4], qga.at[x, j], on_y(j))
    loc_kv = pltpu.make_async_copy(kv.at[y, half], kva.at[c, zl, 0], loc_sem.at[0])
    loc_kv.start()
    loc_qg = pltpu.make_async_copy(qg.at[y], qga.at[x, 0], loc_sem.at[1])
    loc_qg.start()
    rest = pl.ds(1, 3)
    for j in (1, 3, 2):
        got(f"kvy{j}", kva.at[c, zl, j])
    for d in (1, 15, 2, 14):
        send(f"b{d}", kva.at[c, zl, rest], kva.at[c, zl, rest], on_z(d))
    loc_kv.wait()
    send("s0", kva.at[c, zl], kva.at[c, zl], sib)

    def pass_z(part, sl):
        for d in (2, 14):
            zs = (zl + 16 - d) % 8
            got(f"{part}{d}", kva.at[c, zs, sl])
            send(f"{part}3_{d}", kva.at[c, zs, sl], kva.at[c, zs, sl], on_z(1 if d == 2 else 15))
        zs = (zl + 16 - four) % 8
        send(f"{part}4", kva.at[c, zs, sl], kva.at[c, zs, sl], on_z(four))

    def pass_x(j):
        i = 1 if j < 2 else 3
        xs = (x - i + 4) % 4
        got(f"x{i}_{j}", qga.at[xs, j])
        send(f"x2_{j}", qga.at[xs, j], qga.at[xs, j], on_x(i))

    for j in (1, 3, 2):
        got(f"qy{j}", qga.at[x, j])
        for i in (1, 3):
            send(f"x{i}_{j}", qga.at[x, j], qga.at[x, j], on_x(i))
        if j == 1:
            pass_z("a", pl.ds(0, 1))
        if j == 3:
            pass_x(0)

    lane = lax.broadcasted_iota(jnp.int32, (1, RT), 1)
    sub = lax.broadcasted_iota(jnp.int32, (TOK, RT), 0)
    low_lanes = lax.broadcasted_iota(jnp.int32, (RT, WIDE), 1) < HEAD

    def order(n):
        return (zl + jnp.where(n % 2 == 1, (n + 1) // 2, 8 - n // 2)) % 8

    def unpack(n):
        zs = order(n)
        for hf in range(2):
            for j in range(4):
                v = kva[hf, zs, j]
                kvu[zs, TOK * j + 16 * hf : TOK * j + 16 * hf + 16, :] = v[:, :WIDE]
                kvu[zs, TOK * j + 32 + 16 * hf : TOK * j + 48 + 16 * hf, :] = v[:, WIDE:]
        kt[zs] = jnp.transpose(kvu[zs].astype(F32))[:HEAD].astype(BF16)

    def rows_in(xs):
        both = qga[xs].reshape(RT, 2 * WIDE)
        zero = jnp.zeros((RT, WIDE), BF16)
        for m in range(2):
            part = both[:, m * WIDE : (m + 1) * WIDE]
            wq[xs * 2 + m] = jnp.where(low_lanes, part, zero)
            wg[xs * 2 + m] = jnp.where(low_lanes, zero, part)

    def block_of(xs, zs, j):
        return stripe[(xs * 8 + zs) * 4 + (y - j + 4) % 4]

    def rows_of(xs):
        out = jnp.zeros((1, RT), jnp.int32)
        for j in range(4):
            out = jnp.where(lane // TOK == j, block_of(xs, zl, j), out)
        return out

    def tile(xs, row_block, kc, diagonal=False):
        for m in range(2):
            rt = xs * 2 + m
            s = lax.dot_general(kvu[kc], wq[rt], NT, preferred_element_type=F32) * SCALE2
            pg = lax.dot_general(kvu[kc], wg[rt], NT, preferred_element_type=F32)
            pieces, biases = [], []
            top = jnp.full((8, RT), FLOOR, F32)
            for j in range(4):
                piece = s[TOK * j : TOK * (j + 1)]
                key_block = block_of(x, kc, j)
                if diagonal:
                    seen = sub + key_block * TOK <= row_block * TOK + lane % TOK
                    piece = jnp.where(seen, piece, HIDE)
                    bias = jnp.zeros((1, RT), F32)
                else:
                    bias = jnp.where(key_block > row_block, HIDE, 0.0)
                top = jnp.maximum(top, jnp.max(piece.reshape(8, 8, RT), axis=0) + bias)
                pieces.append(piece)
                biases.append(bias)
            top = jnp.max(top, axis=0, keepdims=True)
            total = jnp.zeros((8, RT), F32)
            mixed = jnp.zeros((8, RT), F32)
            for j in range(4):
                e = jnp.exp2(pieces[j] - (top - biases[j]))
                prob[rt, kc, TOK * j : TOK * (j + 1)] = e
                total = total + jnp.sum(e.reshape(8, 8, RT), axis=0)
                mixed = mixed + jnp.sum(
                    (e * pg[TOK * j : TOK * (j + 1)]).reshape(8, 8, RT), axis=0
                )
            grad[rt, kc] = pg
            tile_top[kc, pl.ds(rt, 1)] = top
            tile_sum[kc, pl.ds(rt, 1)] = jnp.sum(total, axis=0, keepdims=True)
            tile_mix[kc, pl.ds(rt, 1)] = jnp.sum(mixed, axis=0, keepdims=True)

    def tiles(xs, lo, hi):
        row_block = rows_of(xs)

        def step(n, _):
            tile(xs, row_block, order(n))
            return 0

        lax.fori_loop(lo, hi, step, 0)

    def unpacks(lo, hi):
        def step(n, _):
            unpack(n)
            return 0

        lax.fori_loop(lo, hi, step, 0)

    loc_qg.wait()
    rows_in(x)
    got("s0", kva.at[1 - c, zl])
    unpack(0)
    tile(x, rows_of(x), zl, True)
    pass_z("b", rest)
    for j in (1, 3, 2):
        pass_x(j)
    for n, d in ((1, 15), (2, 1), (3, 14), (4, 2)):
        zs = order(n)
        if n < 3:
            got(f"a{d}", kva.at[c, zs, pl.ds(0, 1)])
            got(f"b{d}", kva.at[c, zs, rest])
        send(f"s{n}", kva.at[c, zs], kva.at[c, zs], sib)
    for n in range(1, 5):
        got(f"s{n}", kva.at[1 - c, order(n)])
    unpacks(1, 5)
    tiles(x, 1, 5)
    for n, name in ((5, "3_14"), (6, "3_2"), (7, "4")):
        zs = order(n)
        got("a" + name, kva.at[c, zs, pl.ds(0, 1)])
        got("b" + name, kva.at[c, zs, rest])
        send(f"s{n}", kva.at[c, zs], kva.at[c, zs], sib)
    for i in (1, 3):
        xs = (x - i + 4) % 4
        for j in (2, 3) if i == 1 else (0, 1):
            got(f"x{i}_{j}", qga.at[xs, j])
        rows_in(xs)
        tiles(xs, 0, 5)
    for n in range(5, 8):
        got(f"s{n}", kva.at[1 - c, order(n)])
    unpacks(5, 8)

    def late(i, _):
        tiles((x + i + i // 2) % 4, 5, 8)
        return 0

    lax.fori_loop(0, 3, late, 0)
    xs = (x + 2) % 4
    for j in range(4):
        got(f"x2_{j}", qga.at[xs, j])
    rows_in(xs)
    tiles(xs, 0, 8)

    top = tile_top[0]
    for kc in range(1, 8):
        top = jnp.maximum(top, tile_top[kc])
    total = jnp.zeros((8, RT), F32)
    mixed = jnp.zeros((8, RT), F32)
    for kc in range(8):
        up = jnp.exp2(tile_top[kc] - top)
        total = total + tile_sum[kc] * up
        mixed = mixed + tile_mix[kc] * up
    stat[0] = top
    stat[1] = total
    stat[2] = mixed
    for i in (2, 1, 3):
        send(f"st{i}", stat, stat_in.at[i], on_x(i))
    dqt[...] = jnp.zeros_like(dqt)
    for i in (1, 3, 2):
        got(f"st{i}", stat_in.at[i])
    all_top = top
    for i in range(1, 4):
        all_top = jnp.maximum(all_top, stat_in[i, 0])
    up = jnp.exp2(top - all_top)
    total = total * up
    mixed = mixed * up
    for i in range(1, 4):
        up = jnp.exp2(stat_in[i, 0] - all_top)
        total = total + stat_in[i, 1] * up
        mixed = mixed + stat_in[i, 2] * up
    inverse = 1.0 / total
    delta[...] = mixed * inverse
    for kc in range(8):
        fac[kc] = jnp.exp2(tile_top[kc] - all_top) * inverse

    steps = (4, 3, 13, 2, 14, 1, 15, 0)

    def give(k):
        got(f"sb{k}", sbr.at[k])
        total = own[k] + sbr[k].astype(F32)
        if k == 3:
            got("r3", relay.at[0])
            got("r13", relay.at[1])
            got("r4", relay.at[2])
        if k in (3, 4):
            total = total + relay[k - 3].astype(F32)
            far = relay[2].astype(F32)
            total = total + jnp.where(c == k - 3, far, jnp.zeros_like(far))
        l1s[k] = total.astype(BF16)
        if k == 0:
            send("r4", l1s.at[k], relay.at[2], on_z(four))
        elif k < 3:
            send(f"r{steps[k]}", l1s.at[k], relay.at[k - 1], on_z(1 if k == 1 else 15))
        else:
            send(f"f{steps[k]}", l1s.at[k], fin.at[k - 3], on_z(steps[k]))

    for k in range(8):
        kc = (zl + steps[k]) % 8

        def rows_step(rt, dkv):
            p = prob[rt, kc] * fac[kc, pl.ds(rt, 1)]
            ds = (p * (grad[rt, kc] - delta[pl.ds(rt, 1)])).astype(BF16)
            dkv = dkv + dot(p.astype(BF16), wg[rt]) + dot(ds, wq[rt])
            dqt[rt] += dot(kt[kc], ds)
            return dkv

        dkf[...] = lax.fori_loop(0, 8, rows_step, jnp.zeros((RT, WIDE), F32), unroll=8)
        sbs[k] = dkf[pl.ds(pl.multiple_of(128 * (1 - c), 128), 128)].astype(BF16)
        own[k] = dkf[pl.ds(pl.multiple_of(128 * c, 128), 128)]
        send(f"sb{k}", sbs.at[k], sbr.at[k], sib)
        if k >= 2 and k < 7:
            give(k - 2)

    def rows_out(i):
        xs = (x + i) % 4
        pair = dqt[pl.ds(xs * 2, 2)].reshape(WIDE, RT)
        return (jnp.transpose(pair) * SCALE).reshape(4, TOK, WIDE)

    q2s[...] = rows_out(2).astype(BF16)
    send("q2p", q2s.at[pl.ds(0, 2)], q2r.at[0], on_x(1))
    send("q2m", q2s.at[pl.ds(2, 2)], q2r.at[1], on_x(3))
    give(5)
    ahead, back = rows_out(1), rows_out(3)
    q1s[0, 2:] = ahead[2:].astype(BF16)
    q1s[1, :2] = back[:2].astype(BF16)
    send("q1pb", q1s.at[0, pl.ds(2, 2)], q1r.at[0, pl.ds(2, 2)], on_x(1))
    send("q1ma", q1s.at[1, pl.ds(0, 2)], q1r.at[1, pl.ds(0, 2)], on_x(3))
    give(6)
    got("q2p", q2r.at[0])
    q1s[0, :2] = (ahead[:2] + q2r[0].astype(F32)).astype(BF16)
    send("q1pa", q1s.at[0, pl.ds(0, 2)], q1r.at[0, pl.ds(0, 2)], on_x(1))
    got("q2m", q2r.at[1])
    q1s[1, 2:] = (back[2:] + q2r[1].astype(F32)).astype(BF16)
    send("q1mb", q1s.at[1, pl.ds(2, 2)], q1r.at[1, pl.ds(2, 2)], on_x(3))
    mid = rows_out(0)

    got("sb7", sbr.at[7])
    total = own[7] + sbr[7].astype(F32)
    for k in range(3, 7):
        got(f"f{steps[k]}", fin.at[k - 3])
        total = total + fin[k - 3].astype(F32)
    left = lax.broadcasted_iota(jnp.int32, (128, WIDE), 1) < HEAD
    l2s[...] = (total * jnp.where(left, SCALE, 1.0)).astype(BF16).reshape(2, TOK, WIDE)
    head_pair = y // 2
    for q in range(2):
        j = 2 * c + q
        is_self = (c == 0) & (y % 2 == 0) & (q == 0)
        copy = pltpu.make_async_remote_copy(
            src_ref=l2s.at[q], dst_ref=l2r.at[head_pair],
            send_sem=l2_s.at[q], recv_sem=l2_r.at[head_pair],
            device_id=dev(x, (y - j + 4) % 4, z, y % 2), device_id_type=MESH,
        )

        @pl.when(jnp.logical_not(is_self))
        def _():
            copy.start()

        @pl.when(is_self)
        def _():
            l2r[head_pair] = l2s[q]

    got("q1pb", q1r.at[0, pl.ds(2, 2)])
    got("q1ma", q1r.at[1, pl.ds(0, 2)])
    got("q1pa", q1r.at[0, pl.ds(0, 2)])
    got("q1mb", q1r.at[1, pl.ds(2, 2)])
    mid = mid + q1r[0].astype(F32) + q1r[1].astype(F32)
    dqs[...] = mid.astype(BF16)
    for j in (2, 1, 3):
        send(f"dq{j}", dqs.at[j], dq_out.at[y], on_y(4 - j))
    dq_out[y] = dqs[0]

    for hs in range(2):
        is_self = (c == 0) & (y % 2 == 0) & (head_pair == hs)

        @pl.when(jnp.logical_not(is_self))
        def _():
            pltpu.make_async_copy(l2r.at[hs], l2r.at[hs], l2_r.at[hs]).wait()

    send("zz", l2r.at[1 - h], l2z, on_z(8))
    for j in (1, 3, 2):
        got(f"dq{j}", dq_out.at[(y + j) % 4])
    got("zz", l2z)
    dkv_out[...] = (l2r[h].astype(F32) + l2z[...].astype(F32)).astype(BF16)
    for copy in sent:
        copy.wait_send()
    for q in range(2):
        is_self = (c == 0) & (y % 2 == 0) & (q == 0)

        @pl.when(jnp.logical_not(is_self))
        def _():
            pltpu.make_async_copy(l2s.at[q], l2s.at[q], l2_s.at[q]).wait()


def per_device(query_matrix, key_matrix, value_matrix, output_gradient, stripe_map):
    vmem = pl.BlockSpec(memory_space=pltpu.VMEM)
    dma = pltpu.SemaphoreType.DMA
    dq, dkv = pl.pallas_call(
        kernel,
        out_shape=[
            jax.ShapeDtypeStruct((4, TOK, WIDE), BF16),
            jax.ShapeDtypeStruct((TOK, WIDE), BF16),
        ],
        in_specs=[pl.BlockSpec(memory_space=pltpu.SMEM)] + [vmem] * 4,
        out_specs=[vmem, vmem],
        scratch_shapes=[
            pltpu.VMEM((4, TOK, 2 * WIDE), BF16),
            pltpu.VMEM((4, 32, 2 * WIDE), BF16),
            pltpu.VMEM((4, 4, TOK, 2 * WIDE), BF16),
            pltpu.VMEM((2, 8, 4, 16, 2 * WIDE), BF16),
            pltpu.VMEM((8, RT, WIDE), BF16),
            pltpu.VMEM((8, HEAD, RT), BF16),
            pltpu.VMEM((8, RT, WIDE), BF16),
            pltpu.VMEM((8, RT, WIDE), BF16),
            pltpu.VMEM((8, 8, RT, RT), F32),
            pltpu.VMEM((8, 8, RT, RT), F32),
            pltpu.VMEM((8, 8, RT), F32),
            pltpu.VMEM((8, 8, RT), F32),
            pltpu.VMEM((8, 8, RT), F32),
            pltpu.VMEM((3, 8, RT), F32),
            pltpu.VMEM((4, 3, 8, RT), F32),
            pltpu.VMEM((8, 8, RT), F32),
            pltpu.VMEM((8, RT), F32),
            pltpu.VMEM((8, HEAD, RT), F32),
            pltpu.VMEM((RT, WIDE), F32),
            pltpu.VMEM((8, 128, WIDE), F32),
            pltpu.VMEM((8, 128, WIDE), BF16),
            pltpu.VMEM((8, 128, WIDE), BF16),
            pltpu.VMEM((7, 128, WIDE), BF16),
            pltpu.VMEM((3, 128, WIDE), BF16),
            pltpu.VMEM((4, 128, WIDE), BF16),
            pltpu.VMEM((4, TOK, WIDE), BF16),
            pltpu.VMEM((2, 2, TOK, WIDE), BF16),
            pltpu.VMEM((2, 4, TOK, WIDE), BF16),
            pltpu.VMEM((2, 4, TOK, WIDE), BF16),
            pltpu.VMEM((4, TOK, WIDE), BF16),
            pltpu.VMEM((2, TOK, WIDE), BF16),
            pltpu.VMEM((2, TOK, WIDE), BF16),
            pltpu.VMEM((TOK, WIDE), BF16),
            dma((2,)), dma((N_SEM,)), dma((N_SEM,)), dma((2,)), dma((2,)),
        ],
        compiler_params=pltpu.CompilerParams(
            collective_id=0, has_side_effects=True, vmem_limit_bytes=50 * 2**20
        ),
    )(
        stripe_map,
        query_matrix.transpose(1, 0, 2),
        output_gradient.transpose(1, 0, 2),
        key_matrix,
        value_matrix,
    )
    return dq.transpose(1, 0, 2), dkv[:, :HEAD], dkv[:, HEAD:]


def solution(mesh):
    return jax.shard_map(
        per_device,
        mesh=mesh,
        in_specs=(
            P(("blk", "uly"), None, "tp"),
            P(("blk", "uly"), None),
            P(("blk", "uly"), None),
            P(("blk", "uly"), None, "tp"),
            P(),
        ),
        out_specs=(P(("blk", "uly"), None, "tp"), P(("blk", "uly"), "tp"), P(("blk", "uly"), "tp")),
        check_vma=False,
    )
```

time: 83.8 us -> 79.9 us (0.953)
  local copies, waits for them, and re-layouts: 8.22 us -> 3.1 us
  Pallas kernels: 73.5 us -> 76 us
  other arithmetic: 1.05 us -> 0 us
    reshape x10 -> x0, local copies, waits for them, and re-layouts: 3.77 us -> none  [the longest x2 1.33 us: per_device(): q = query_matrix.reshape(TOK, 4, 2, 1, HEAD)]
    pallas_call x1, Pallas kernels: 73.5 us -> 76 us  [per_device(): pl.pallas_call(kernel, out_shape=[jax.ShapeDtypeStruct((4, TOK, WIDE), BF...]
    unnamed x7, local copies, waits for them, and re-layouts: 2.97 us -> 1.4 us
    transpose x0 -> x1, local copies, waits for them, and re-layouts: none -> 1.02 us  [per_device(): output_gradient.transpose(1, 0, 2)]
where the time goes in v2:
time: 79.9 us; the launch traced here: 79.8 us
  Pallas kernels  76 us (95%)
  local copies, waits for them, and re-layouts  3.1 us (4%)
    pallas_call x1, Pallas kernels, per_device(): pl.pallas_call(kernel, out_shape=[jax.ShapeDtypeStruct((4, TOK, WIDE), BF...  76 us

profile of v2, /device:TPU:1, one launch (start us, length us, event | category | flops | bytes accessed | tf_op | source)
XLA Modules:
  0.0 79.8 jit_solution(14098194111006741108)
XLA Ops:
  0.6 0.0 copy-start.1
  0.6 0.0 copy-start
  0.7 1.0 %copy_bitcast_fusion = (bf16[4,64,192]{2,1,0:T(8,128)(2,1)S(1)}, bf16[4,64,192]{2,1,0:T(8,128)(2,1)S(1)}) fusion(bf16[64,4,192]{2,1,0:T(4,128)(2,1)} %param.8, bf16[64,4,192]{2,1,0:T(4,128)(2,1)} %param.5), kind=kLoop, calls=%fused_computation | loop fusion | bytes 393216 | tf_op jit(solution)/shard_map/transpose | solution.py:461
  1.7 0.0 copy-start.2
  1.7 0.0 copy-done.1
  1.7 0.0 copy-done
  1.7 0.6 copy-done.2
  2.3 76.0 %shard_map.76 = (bf16[4,64,192]{2,1,0:T(8,128)(2,1)S(1)}, bf16[64,192]{1,0:T(8,128)(2,1)S(1)}) custom-call(s32[128]{0:T(128)S(1)} %copy-done.2, bf16[4,64,192]{2,1,0:T(8,128)(2,1)S(1)} %get-tuple-element.13.q_in, bf16[4,64,192]{2,1,0:T(8,128)(2,1)S(1)} %get-tuple-element.12.g_in, bf16[64,384]{1,0:T(8,128)(2,1)S(1)} %copy-done, bf16[64,384]{1,0:T(8,128)(2,1)S(1)} %copy-done.1), custom_call_target="tpu_custom_call" | custom-call | tf_op jit(solution)/shard_map/pallas_call | solution.py:411
  78.3 0.8 copy.10
  79.1 0.7 fusion
Async XLA Ops:
  0.6 1.1 %copy-start.1 = (bf16[64,384]{1,0:T(8,128)(2,1)S(1)}, bf16[64,384]{1,0:T(8,128)(2,1)}, u32[]{:S(2)}) copy-start(bf16[64,384]{1,0:T(8,128)(2,1)} %v_in.1) | copy-start | bytes 147460
  0.6 1.1 %copy-start = (bf16[64,384]{1,0:T(8,128)(2,1)S(1)}, bf16[64,384]{1,0:T(8,128)(2,1)}, u32[]{:S(2)}) copy-start(bf16[64,384]{1,0:T(8,128)(2,1)} %k_in.1) | copy-start | bytes 147460
  1.7 0.7 copy-start.2

commit v3 on v2

v3 whole, which is shorter than its diff:
```python
import jax
import jax.numpy as jnp
from jax import lax
from jax.experimental import pallas as pl
from jax.experimental.pallas import tpu as pltpu
from jax.sharding import PartitionSpec as P

HEAD = 96
WIDE = 2 * HEAD
TOK = 64
RT = 256
LOG2E = 1.4426950408889634
SCALE = HEAD**-0.5
SCALE2 = SCALE * LOG2E
HIDE = -1e30
FLOOR = -1e29
F32 = jnp.float32
BF16 = jnp.bfloat16
MESH = pl.DeviceIdType.MESH
NT = (((1,), (1,)), ((), ()))
N_SEM = 96


def dot(a, b):
    return jnp.dot(a, b, preferred_element_type=F32)


def kernel(
    stripe, q_in, g_in, k_in, v_in, dq_out, dkv_out,
    qg, kv, qga, kva, kvu, kt, wq, wg, prob, grad,
    tile_top, tile_sum, tile_mix, stat, stat_in, fac, delta,
    dqt, dkf, own, sbs, sbr, l1s, fin, dqb, dqr, l2s, l2r,
    loc_sem, send_sem, recv_sem, l2_s, l2_r,
):
    b, y, t = lax.axis_index("blk"), lax.axis_index("uly"), lax.axis_index("tp")
    x, zl = b // 8, b % 8
    h, c = t // 2, t % 2
    z = h * 8 + zl

    def dev(x_, y_, z_, c_):
        return (x_ * 8 + z_ % 8, y_, (z_ // 8) * 2 + c_)

    def on_x(i):
        return dev((x + i) % 4, y, z, c)

    def on_y(j):
        return dev(x, (y + j) % 4, z, c)

    def on_z(d):
        return dev(x, y, (z + d) % 16, c)

    sib = dev(x, y, z, 1 - c)
    zsteps = (0, 1, 15, 2, 14, 3, 13, jnp.where(c == 0, 4, 12))
    sent = []
    names = {}

    def send(name, src, dst, to):
        n = names.setdefault(name, len(names))
        copy = pltpu.make_async_remote_copy(
            src_ref=src, dst_ref=dst, send_sem=send_sem.at[n], recv_sem=recv_sem.at[n],
            device_id=to, device_id_type=MESH,
        )
        copy.start()
        sent.append(copy)

    def got(name, ref):
        pltpu.make_async_copy(ref, ref, recv_sem.at[names[name]]).wait()

    barrier = pltpu.get_barrier_semaphore()
    peers = [dev((x + i) % 4, (y + j) % 4, z, c) for i in range(4) for j in range(4) if i or j]
    peers += [
        dev(x, (y + j) % 4, (z + d) % 16, c) for d in (1, 15, 2, 14, 3, 13, 4, 12) for j in range(4)
    ]
    peers += [sib]

    def greet(to):
        pl.semaphore_signal(barrier, inc=1, device_id=to, device_id_type=MESH)

    for to in peers:
        greet(to)
    mine = (c == 0) & (y % 2 == 0) & (h == y // 2)
    for hs in range(2):

        @pl.when(jnp.logical_not(mine & (h == hs)))
        def _():
            greet(dev(x, t, hs * 8 + zl, ((t - y + 4) % 4) // 2))

    for g in range(4):
        part = slice(g * HEAD, (g + 1) * HEAD)
        kv[g] = jnp.concatenate(
            [k_in[:32, part], v_in[:32, part], k_in[32:, part], v_in[32:, part]], axis=1
        )
        qs, gs = q_in[g], g_in[g]
        qg[g] = jnp.concatenate(
            [qs[:, :HEAD], gs[:, :HEAD], qs[:, HEAD:], gs[:, HEAD:]], axis=1
        )
    pl.semaphore_wait(barrier, len(peers) + 2 - jnp.where(mine, 1, 0))

    half = pl.ds(pl.multiple_of(16 * c, 16), 16)

    def send_kv(n, j):
        send(
            f"k{n}_{j}", kv.at[(y + j) % 4, half], kva.at[c, zl, j],
            dev(x, (y + j) % 4, (z + zsteps[n]) % 16, c),
        )

    loc_kv = pltpu.make_async_copy(kv.at[y, half], kva.at[c, zl, 0], loc_sem.at[0])
    loc_kv.start()
    loc_qg = pltpu.make_async_copy(qg.at[y], qga.at[x, 0], loc_sem.at[1])
    loc_qg.start()
    for j in (1, 3, 2):
        send_kv(0, j)
    for j in (1, 3, 2):
        send(f"qy{j}", qg.at[(y + j) % 4], qga.at[x, j], on_y(j))
    for i in (1, 3, 2):
        send(f"x{i}_0", qg.at[y], qga.at[x, 0], on_x(i))
    for n in range(1, 8):
        for j in (0, 1, 3, 2):
            send_kv(n, j)

    def share_kv(n):
        zs = (zl + 16 - zsteps[n]) % 8
        for j in range(4):
            if n or j:
                got(f"k{n}_{j}", kva.at[c, zs, j])
        send(f"s{n}", kva.at[c, zs], kva.at[c, zs], sib)

    loc_kv.wait()
    share_kv(0)
    for j in (1, 3, 2):
        got(f"qy{j}", qga.at[x, j])
        for i in (1, 3):
            send(f"x{i}_{j}", qga.at[x, j], qga.at[x, j], on_x(i))
    for j in (1, 3, 2):
        send(f"x2_{j}", qga.at[x, j], qga.at[x, j], on_x(2))

    lane = lax.broadcasted_iota(jnp.int32, (1, RT), 1)
    sub = lax.broadcasted_iota(jnp.int32, (TOK, RT), 0)
    low_lanes = lax.broadcasted_iota(jnp.int32, (RT, WIDE), 1) < HEAD

    def order(n):
        return (zl + jnp.where(n % 2 == 1, 8 - (n + 1) // 2, n // 2)) % 8

    def unpack(n):
        zs = order(n)
        for hf in range(2):
            for j in range(4):
                v = kva[hf, zs, j]
                kvu[zs, TOK * j + 16 * hf : TOK * j + 16 * hf + 16, :] = v[:, :WIDE]
                kvu[zs, TOK * j + 32 + 16 * hf : TOK * j + 48 + 16 * hf, :] = v[:, WIDE:]

    def rows_in(xs):
        both = qga[xs].reshape(RT, 2 * WIDE)
        zero = jnp.zeros((RT, WIDE), BF16)
        for m in range(2):
            part = both[:, m * WIDE : (m + 1) * WIDE]
            wq[xs * 2 + m] = jnp.where(low_lanes, part, zero)
            wg[xs * 2 + m] = jnp.where(low_lanes, zero, part)

    def block_of(xs, zs, j):
        return stripe[(xs * 8 + zs) * 4 + (y - j + 4) % 4]

    def rows_of(xs):
        out = jnp.zeros((1, RT), jnp.int32)
        for j in range(4):
            out = jnp.where(lane // TOK == j, block_of(xs, zl, j), out)
        return out

    def tile(xs, row_block, kc, diagonal=False):
        for m in range(2):
            rt = xs * 2 + m
            s = lax.dot_general(kvu[kc], wq[rt], NT, preferred_element_type=F32) * SCALE2
            pg = lax.dot_general(kvu[kc], wg[rt], NT, preferred_element_type=F32)
            pieces, biases = [], []
            top = jnp.full((8, RT), FLOOR, F32)
            for j in range(4):
                piece = s[TOK * j : TOK * (j + 1)]
                key_block = block_of(x, kc, j)
                if diagonal:
                    seen = sub + key_block * TOK <= row_block * TOK + lane % TOK
                    piece = jnp.where(seen, piece, HIDE)
                    bias = jnp.zeros((1, RT), F32)
                else:
                    bias = jnp.where(key_block > row_block, HIDE, 0.0)
                top = jnp.maximum(top, jnp.max(piece.reshape(8, 8, RT), axis=0) + bias)
                pieces.append(piece)
                biases.append(bias)
            top = jnp.max(top, axis=0, keepdims=True)
            total = jnp.zeros((8, RT), F32)
            mixed = jnp.zeros((8, RT), F32)
            for j in range(4):
                e = jnp.exp2(pieces[j] - (top - biases[j]))
                prob[rt, kc, TOK * j : TOK * (j + 1)] = e
                total = total + jnp.sum(e.reshape(8, 8, RT), axis=0)
                mixed = mixed + jnp.sum(
                    (e * pg[TOK * j : TOK * (j + 1)]).reshape(8, 8, RT), axis=0
                )
            grad[rt, kc] = pg
            tile_top[kc, pl.ds(rt, 1)] = top
            tile_sum[kc, pl.ds(rt, 1)] = jnp.sum(total, axis=0, keepdims=True)
            tile_mix[kc, pl.ds(rt, 1)] = jnp.sum(mixed, axis=0, keepdims=True)

    def tiles(xs, lo, count, turns=1):
        row_block = rows_of(xs)

        def step(turn, _):
            for n in range(count):
                tile(xs, row_block, order(lo + turn * count + n))
            return 0

        lax.fori_loop(0, turns, step, 0)

    loc_qg.wait()
    rows_in(x)
    got("s0", kva.at[1 - c, zl])
    unpack(0)
    tile(x, rows_of(x), zl, True)
    for lo, count in ((1, 4), (5, 3)):
        for n in range(lo, lo + count):
            share_kv(n)
        for n in range(lo, lo + count):
            got(f"s{n}", kva.at[1 - c, order(n)])
            unpack(n)
        tiles(x, lo, count)
    for i in (1, 3, 2):
        xs = (x - i + 4) % 4
        for j in range(4):
            got(f"x{i}_{j}", qga.at[xs, j])
        rows_in(xs)
        tiles(xs, 0, 4, 2)

    top = tile_top[0]
    for kc in range(1, 8):
        top = jnp.maximum(top, tile_top[kc])
    total = jnp.zeros((8, RT), F32)
    mixed = jnp.zeros((8, RT), F32)
    for kc in range(8):
        up = jnp.exp2(tile_top[kc] - top)
        total = total + tile_sum[kc] * up
        mixed = mixed + tile_mix[kc] * up
    stat[0] = top
    stat[1] = total
    stat[2] = mixed
    for i in (2, 1, 3):
        send(f"st{i}", stat, stat_in.at[i], on_x(i))
    dqt[...] = jnp.zeros_like(dqt)

    def turn_keys(kc, _):
        kt[kc] = jnp.transpose(kvu[kc].astype(F32))[:HEAD].astype(BF16)
        return 0

    lax.fori_loop(0, 8, turn_keys, 0)
    for i in (1, 3, 2):
        got(f"st{i}", stat_in.at[i])
    all_top = top
    for i in range(1, 4):
        all_top = jnp.maximum(all_top, stat_in[i, 0])
    up = jnp.exp2(top - all_top)
    total = total * up
    mixed = mixed * up
    for i in range(1, 4):
        up = jnp.exp2(stat_in[i, 0] - all_top)
        total = total + stat_in[i, 1] * up
        mixed = mixed + stat_in[i, 2] * up
    inverse = 1.0 / total
    delta[...] = mixed * inverse
    for kc in range(8):
        fac[kc] = jnp.exp2(tile_top[kc] - all_top) * inverse

    steps = (zsteps[7], 3, 13, 2, 14, 1, 15, 0)

    def give(k):
        got(f"sb{k}", sbr.at[k])
        l1s[k] = (own[k] + sbr[k].astype(F32)).astype(BF16)
        send(f"f{k}", l1s.at[k], fin.at[k], on_z(steps[k]))

    for k in range(8):
        kc = (zl + steps[k]) % 8

        def rows_step(rt, dkv):
            p = prob[rt, kc] * fac[kc, pl.ds(rt, 1)]
            ds = (p * (grad[rt, kc] - delta[pl.ds(rt, 1)])).astype(BF16)
            dkv = dkv + dot(p.astype(BF16), wg[rt]) + dot(ds, wq[rt])
            dqt[rt] += dot(kt[kc], ds)
            return dkv

        dkf[...] = lax.fori_loop(0, 8, rows_step, jnp.zeros((RT, WIDE), F32), unroll=8)
        sbs[k] = dkf[pl.ds(pl.multiple_of(128 * (1 - c), 128), 128)].astype(BF16)
        own[k] = dkf[pl.ds(pl.multiple_of(128 * c, 128), 128)]
        send(f"sb{k}", sbs.at[k], sbr.at[k], sib)
        if k >= 2 and k < 7:
            give(k - 2)

    give(5)
    for i in (2, 1, 3, 0):
        xs = (x + i) % 4
        pair = dqt[pl.ds(xs * 2, 2)].reshape(WIDE, RT)
        dqb[i] = (jnp.transpose(pair) * SCALE).astype(BF16).reshape(4, TOK, WIDE)
        for j in (2, 1, 3, 0):
            if i or j:
                send(
                    f"dq{i}_{j}", dqb.at[i, j], dqr.at[i, y],
                    dev(xs, (y - j + 4) % 4, z, c),
                )
        if i == 2:
            give(6)
    dqr[0, y] = dqb[0, 0]

    got("sb7", sbr.at[7])
    total = own[7] + sbr[7].astype(F32)
    for k in range(7):
        got(f"f{k}", fin.at[k])
        total = total + fin[k].astype(F32)
    left = lax.broadcasted_iota(jnp.int32, (128, WIDE), 1) < HEAD
    l2s[...] = (total * jnp.where(left, SCALE, 1.0)).astype(BF16).reshape(2, TOK, WIDE)
    for q in range(2):
        j = 2 * c + q
        yo = (y - j + 4) % 4
        is_self = mine & (yo == y)
        copy = pltpu.make_async_remote_copy(
            src_ref=l2s.at[q], dst_ref=l2r.at[h], send_sem=l2_s.at[q], recv_sem=l2_r.at[h],
            device_id=dev(x, yo, 8 * (y // 2) + zl, y % 2), device_id_type=MESH,
        )

        @pl.when(jnp.logical_not(is_self))
        def _():
            copy.start()

        @pl.when(is_self)
        def _():
            l2r[h] = l2s[q]

    for j in range(4):
        gs = (y + j) % 4
        total = jnp.zeros((TOK, WIDE), F32)
        for i in (0, 1, 3, 2):
            if i or j:
                got(f"dq{i}_{j}", dqr.at[i, gs])
            total = total + dqr[i, gs].astype(F32)
        dq_out[gs] = total.astype(BF16)

    for hs in range(2):

        @pl.when(jnp.logical_not(mine & (h == hs)))
        def _():
            pltpu.make_async_copy(l2r.at[hs], l2r.at[hs], l2_r.at[hs]).wait()

    dkv_out[...] = (l2r[0].astype(F32) + l2r[1].astype(F32)).astype(BF16)
    for copy in sent:
        copy.wait_send()
    for q in range(2):
        yo = (y - 2 * c - q + 4) % 4

        @pl.when(jnp.logical_not(mine & (yo == y)))
        def _():
            pltpu.make_async_copy(l2s.at[q], l2s.at[q], l2_s.at[q]).wait()


def per_device(query_matrix, key_matrix, value_matrix, output_gradient, stripe_map):
    vmem = pl.BlockSpec(memory_space=pltpu.VMEM)
    dma = pltpu.SemaphoreType.DMA
    dq, dkv = pl.pallas_call(
        kernel,
        out_shape=[
            jax.ShapeDtypeStruct((4, TOK, WIDE), BF16),
            jax.ShapeDtypeStruct((TOK, WIDE), BF16),
        ],
        in_specs=[pl.BlockSpec(memory_space=pltpu.SMEM)] + [vmem] * 4,
        out_specs=[vmem, vmem],
        scratch_shapes=[
            pltpu.VMEM((4, TOK, 2 * WIDE), BF16),
            pltpu.VMEM((4, 32, 2 * WIDE), BF16),
            pltpu.VMEM((4, 4, TOK, 2 * WIDE), BF16),
            pltpu.VMEM((2, 8, 4, 16, 2 * WIDE), BF16),
            pltpu.VMEM((8, RT, WIDE), BF16),
            pltpu.VMEM((8, HEAD, RT), BF16),
            pltpu.VMEM((8, RT, WIDE), BF16),
            pltpu.VMEM((8, RT, WIDE), BF16),
            pltpu.VMEM((8, 8, RT, RT), F32),
            pltpu.VMEM((8, 8, RT, RT), F32),
            pltpu.VMEM((8, 8, RT), F32),
            pltpu.VMEM((8, 8, RT), F32),
            pltpu.VMEM((8, 8, RT), F32),
            pltpu.VMEM((3, 8, RT), F32),
            pltpu.VMEM((4, 3, 8, RT), F32),
            pltpu.VMEM((8, 8, RT), F32),
            pltpu.VMEM((8, RT), F32),
            pltpu.VMEM((8, HEAD, RT), F32),
            pltpu.VMEM((RT, WIDE), F32),
            pltpu.VMEM((8, 128, WIDE), F32),
            pltpu.VMEM((8, 128, WIDE), BF16),
            pltpu.VMEM((8, 128, WIDE), BF16),
            pltpu.VMEM((7, 128, WIDE), BF16),
            pltpu.VMEM((7, 128, WIDE), BF16),
            pltpu.VMEM((4, 4, TOK, WIDE), BF16),
            pltpu.VMEM((4, 4, TOK, WIDE), BF16),
            pltpu.VMEM((2, TOK, WIDE), BF16),
            pltpu.VMEM((2, TOK, WIDE), BF16),
            dma((2,)), dma((N_SEM,)), dma((N_SEM,)), dma((2,)), dma((2,)),
        ],
        compiler_params=pltpu.CompilerParams(
            collective_id=0, has_side_effects=True, vmem_limit_bytes=50 * 2**20
        ),
    )(
        stripe_map,
        query_matrix.transpose(1, 0, 2),
        output_gradient.transpose(1, 0, 2),
        key_matrix,
        value_matrix,
    )
    return dq.transpose(1, 0, 2), dkv[:, :HEAD], dkv[:, HEAD:]


def solution(mesh):
    return jax.shard_map(
        per_device,
        mesh=mesh,
        in_specs=(
            P(("blk", "uly"), None, "tp"),
            P(("blk", "uly"), None),
            P(("blk", "uly"), None),
            P(("blk", "uly"), None, "tp"),
            P(),
        ),
        out_specs=(P(("blk", "uly"), None, "tp"), P(("blk", "uly"), "tp"), P(("blk", "uly"), "tp")),
        check_vma=False,
    )
```

time: 79.9 us -> 77.1 us (0.965)
  the two profiles are of different devices: /device:TPU:1 before, /device:TPU:33 now
where the time goes in v3:
time: 77.1 us; the launch traced here: 77 us
  Pallas kernels  73.2 us (95%)
  local copies, waits for them, and re-layouts  3.1 us (4%)
    pallas_call x1, Pallas kernels, per_device(): pl.pallas_call(kernel, out_shape=[jax.ShapeDtypeStruct((4, TOK, WIDE), BF...  73.2 us

profile of v3, /device:TPU:33, one launch (start us, length us, event | category | flops | bytes accessed | tf_op | source)
XLA Modules:
  0.0 77.0 jit_solution(8280320710888445641)
XLA Ops:
  0.6 0.0 copy-start.1
  0.6 0.0 copy-start
  0.7 1.0 %copy_bitcast_fusion = (bf16[4,64,192]{2,1,0:T(8,128)(2,1)S(1)}, bf16[4,64,192]{2,1,0:T(8,128)(2,1)S(1)}) fusion(bf16[64,4,192]{2,1,0:T(4,128)(2,1)} %param.8, bf16[64,4,192]{2,1,0:T(4,128)(2,1)} %param.5), kind=kLoop, calls=%fused_computation | loop fusion | bytes 393216 | tf_op jit(solution)/shard_map/transpose | solution.py:407
  1.7 0.0 copy-start.2
  1.7 0.0 copy-done.1
  1.7 0.0 copy-done
  1.7 0.6 copy-done.2
  2.3 73.2 %shard_map.76 = (bf16[4,64,192]{2,1,0:T(8,128)(2,1)S(1)}, bf16[64,192]{1,0:T(8,128)(2,1)S(1)}) custom-call(s32[128]{0:T(128)S(1)} %copy-done.2, bf16[4,64,192]{2,1,0:T(8,128)(2,1)S(1)} %get-tuple-element.13.q_in, bf16[4,64,192]{2,1,0:T(8,128)(2,1)S(1)} %get-tuple-element.12.g_in, bf16[64,384]{1,0:T(8,128)(2,1)S(1)} %copy-done, bf16[64,384]{1,0:T(8,128)(2,1)S(1)} %copy-done.1), custom_call_target="tpu_custom_call" | custom-call | tf_op jit(solution)/shard_map/pallas_call | solution.py:362
  75.5 0.8 copy.10
  76.3 0.7 fusion
Async XLA Ops:
  0.6 1.1 %copy-start.1 = (bf16[64,384]{1,0:T(8,128)(2,1)S(1)}, bf16[64,384]{1,0:T(8,128)(2,1)}, u32[]{:S(2)}) copy-start(bf16[64,384]{1,0:T(8,128)(2,1)} %v_in.1) | copy-start | bytes 147460
  0.6 1.1 %copy-start = (bf16[64,384]{1,0:T(8,128)(2,1)S(1)}, bf16[64,384]{1,0:T(8,128)(2,1)}, u32[]{:S(2)}) copy-start(bf16[64,384]{1,0:T(8,128)(2,1)} %k_in.1) | copy-start | bytes 147460
  1.7 0.7 copy-start.2

commit v4 on v3

--- a/solution.py
+++ b/solution.py
@@ -29,7 +29,7 @@
     stripe, q_in, g_in, k_in, v_in, dq_out, dkv_out,
     qg, kv, qga, kva, kvu, kt, wq, wg, prob, grad,
     tile_top, tile_sum, tile_mix, stat, stat_in, fac, delta,
-    dqt, dkf, own, sbs, sbr, l1s, fin, dqb, dqr, l2s, l2r,
+    dqt, dkf, own, sbs, sbr, l1s, relay, fin, dqb, dqr, l2s, l2r,
     loc_sem, send_sem, recv_sem, l2_s, l2_r,
 ):
     b, y, t = lax.axis_index("blk"), lax.axis_index("uly"), lax.axis_index("tp")
@@ -68,9 +68,8 @@
 
     barrier = pltpu.get_barrier_semaphore()
     peers = [dev((x + i) % 4, (y + j) % 4, z, c) for i in range(4) for j in range(4) if i or j]
-    peers += [
-        dev(x, (y + j) % 4, (z + d) % 16, c) for d in (1, 15, 2, 14, 3, 13, 4, 12) for j in range(4)
-    ]
+    peers += [on_z(d) for d in (1, 15, 2, 14)]
+    peers += [dev(x, (y + j) % 4, (z + d) % 16, c) for d in (3, 13, 4, 12) for j in range(4)]
     peers += [sib]
 
     def greet(to):
@@ -112,17 +111,32 @@
         send_kv(0, j)
     for j in (1, 3, 2):
         send(f"qy{j}", qg.at[(y + j) % 4], qga.at[x, j], on_y(j))
-    for i in (1, 3, 2):
+    for i in (1, 3):
         send(f"x{i}_0", qg.at[y], qga.at[x, 0], on_x(i))
-    for n in range(1, 8):
+    for n in (7, 5, 6):
         for j in (0, 1, 3, 2):
             send_kv(n, j)
+    for n in range(1, 5):
+        send_kv(n, 0)
+    for j in (0, 1, 3, 2):
+        send(
+            f"x2_{j}", qg.at[(y + j) % 4], qga.at[x, j],
+            dev((x + 2) % 4, (y + j) % 4, z, c),
+        )
+    rest = pl.ds(1, 3)
 
     def share_kv(n):
         zs = (zl + 16 - zsteps[n]) % 8
-        for j in range(4):
-            if n or j:
-                got(f"k{n}_{j}", kva.at[c, zs, j])
+        if 0 < n < 5:
+            got(f"k{n}_0", kva.at[c, zs, 0])
+            got(f"k{n}_r", kva.at[c, zs, rest])
+        else:
+            for j in range(4):
+                if n or j:
+                    got(f"k{n}_{j}", kva.at[c, zs, j])
+        if n == 0:
+            for d in range(1, 5):
+                send(f"k{d}_r", kva.at[c, zl, rest], kva.at[c, zl, rest], on_z(zsteps[d]))
         send(f"s{n}", kva.at[c, zs], kva.at[c, zs], sib)
 
     loc_kv.wait()
@@ -131,8 +145,6 @@
         got(f"qy{j}", qga.at[x, j])
         for i in (1, 3):
             send(f"x{i}_{j}", qga.at[x, j], qga.at[x, j], on_x(i))
-    for j in (1, 3, 2):
-        send(f"x2_{j}", qga.at[x, j], qga.at[x, j], on_x(2))
 
     lane = lax.broadcasted_iota(jnp.int32, (1, RT), 1)
     sub = lax.broadcasted_iota(jnp.int32, (TOK, RT), 0)
@@ -271,8 +283,22 @@
 
     def give(k):
         got(f"sb{k}", sbr.at[k])
-        l1s[k] = (own[k] + sbr[k].astype(F32)).astype(BF16)
-        send(f"f{k}", l1s.at[k], fin.at[k], on_z(steps[k]))
+        total = own[k] + sbr[k].astype(F32)
+        if k in (3, 4):
+            got(f"r{k - 2}", relay.at[k - 2])
+            if k == 3:
+                got("r0", relay.at[0])
+            far = relay[0].astype(F32)
+            total = total + relay[k - 2].astype(F32)
+            total = total + jnp.where(c == k - 3, far, jnp.zeros_like(far))
+        l1s[k] = total.astype(BF16)
+        if k < 3:
+            send(f"r{k}", l1s.at[k], relay.at[k], on_z((jnp.where(c == 0, 2, 14), 1, 15)[k]))
+        else:
+            send(f"f{k}", l1s.at[k], fin.at[k - 3], on_z(steps[k]))
+
+    def packed(rows):
+        return jnp.concatenate([rows[:TOK], rows[TOK:]], axis=1)
 
     for k in range(8):
         kc = (zl + steps[k]) % 8
@@ -285,17 +311,17 @@
             return dkv
 
         dkf[...] = lax.fori_loop(0, 8, rows_step, jnp.zeros((RT, WIDE), F32), unroll=8)
-        sbs[k] = dkf[pl.ds(pl.multiple_of(128 * (1 - c), 128), 128)].astype(BF16)
-        own[k] = dkf[pl.ds(pl.multiple_of(128 * c, 128), 128)]
+        sbs[k] = packed(dkf[pl.ds(pl.multiple_of(128 * (1 - c), 128), 128)]).astype(BF16)
+        own[k] = packed(dkf[pl.ds(pl.multiple_of(128 * c, 128), 128)])
         send(f"sb{k}", sbs.at[k], sbr.at[k], sib)
-        if k >= 2 and k < 7:
+        if k in (2, 3, 4, 7):
             give(k - 2)
 
-    give(5)
     for i in (2, 1, 3, 0):
         xs = (x + i) % 4
         pair = dqt[pl.ds(xs * 2, 2)].reshape(WIDE, RT)
-        dqb[i] = (jnp.transpose(pair) * SCALE).astype(BF16).reshape(4, TOK, WIDE)
+        rows = (jnp.transpose(pair) * SCALE).reshape(4, TOK, WIDE)
+        dqb[i] = jnp.concatenate([rows[:, :32], rows[:, 32:]], axis=2).astype(BF16)
         for j in (2, 1, 3, 0):
             if i or j:
                 send(
@@ -304,15 +330,19 @@
                 )
         if i == 2:
             give(6)
+        if i == 1:
+            give(3)
+            give(4)
     dqr[0, y] = dqb[0, 0]
 
     got("sb7", sbr.at[7])
     total = own[7] + sbr[7].astype(F32)
-    for k in range(7):
-        got(f"f{k}", fin.at[k])
-        total = total + fin[k].astype(F32)
-    left = lax.broadcasted_iota(jnp.int32, (128, WIDE), 1) < HEAD
-    l2s[...] = (total * jnp.where(left, SCALE, 1.0)).astype(BF16).reshape(2, TOK, WIDE)
+    for k in range(3, 7):
+        got(f"f{k}", fin.at[k - 3])
+        total = total + fin[k - 3].astype(F32)
+    left = lax.broadcasted_iota(jnp.int32, (TOK, WIDE), 1) < HEAD
+    for q in range(2):
+        l2s[q] = (total[:, q * WIDE : (q + 1) * WIDE] * jnp.where(left, SCALE, 1.0)).astype(BF16)
     for q in range(2):
         j = 2 * c + q
         yo = (y - j + 4) % 4
@@ -332,12 +362,13 @@
 
     for j in range(4):
         gs = (y + j) % 4
-        total = jnp.zeros((TOK, WIDE), F32)
+        total = jnp.zeros((32, 2 * WIDE), F32)
         for i in (0, 1, 3, 2):
             if i or j:
                 got(f"dq{i}_{j}", dqr.at[i, gs])
             total = total + dqr[i, gs].astype(F32)
-        dq_out[gs] = total.astype(BF16)
+        dq_out[gs, :32] = total[:, :WIDE].astype(BF16)
+        dq_out[gs, 32:] = total[:, WIDE:].astype(BF16)
 
     for hs in range(2):
 
@@ -387,13 +418,14 @@
             pltpu.VMEM((8, RT), F32),
             pltpu.VMEM((8, HEAD, RT), F32),
             pltpu.VMEM((RT, WIDE), F32),
-            pltpu.VMEM((8, 128, WIDE), F32),
-            pltpu.VMEM((8, 128, WIDE), BF16),
-            pltpu.VMEM((8, 128, WIDE), BF16),
-            pltpu.VMEM((7, 128, WIDE), BF16),
-            pltpu.VMEM((7, 128, WIDE), BF16),
-            pltpu.VMEM((4, 4, TOK, WIDE), BF16),
-            pltpu.VMEM((4, 4, TOK, WIDE), BF16),
+            pltpu.VMEM((8, TOK, 2 * WIDE), F32),
+            pltpu.VMEM((8, TOK, 2 * WIDE), BF16),
+            pltpu.VMEM((8, TOK, 2 * WIDE), BF16),
+            pltpu.VMEM((7, TOK, 2 * WIDE), BF16),
+            pltpu.VMEM((3, TOK, 2 * WIDE), BF16),
+            pltpu.VMEM((4, TOK, 2 * WIDE), BF16),
+            pltpu.VMEM((4, 4, 32, 2 * WIDE), BF16),
+            pltpu.VMEM((4, 4, 32, 2 * WIDE), BF16),
             pltpu.VMEM((2, TOK, WIDE), BF16),
             pltpu.VMEM((2, TOK, WIDE), BF16),
             dma((2,)), dma((N_SEM,)), dma((N_SEM,)), dma((2,)), dma((2,)),

time: 77.1 us -> 73.5 us (0.953)
  the two profiles are of different devices: /device:TPU:33 before, /device:TPU:1 now
where the time goes in v4:
time: 73.5 us; the launch traced here: 72.8 us
  Pallas kernels  69 us (94%)
  local copies, waits for them, and re-layouts  3.1 us (4%)
    pallas_call x1, Pallas kernels, per_device(): pl.pallas_call(kernel, out_shape=[jax.ShapeDtypeStruct((4, TOK, WIDE), BF...  69 us

profile of v4, /device:TPU:1, one launch (start us, length us, event | category | flops | bytes accessed | tf_op | source)
XLA Modules:
  0.0 72.8 jit_solution(18080278329956286029)
XLA Ops:
  0.6 0.0 copy-start.1
  0.6 0.0 copy-start
  0.7 1.0 %copy_bitcast_fusion = (bf16[4,64,192]{2,1,0:T(8,128)(2,1)S(1)}, bf16[4,64,192]{2,1,0:T(8,128)(2,1)S(1)}) fusion(bf16[64,4,192]{2,1,0:T(4,128)(2,1)} %param.8, bf16[64,4,192]{2,1,0:T(4,128)(2,1)} %param.5), kind=kLoop, calls=%fused_computation | loop fusion | bytes 393216 | tf_op jit(solution)/shard_map/transpose | solution.py:439
  1.7 0.0 copy-start.2
  1.7 0.0 copy-done.1
  1.7 0.0 copy-done
  1.7 0.6 copy-done.2
  2.3 69.0 %shard_map.76 = (bf16[4,64,192]{2,1,0:T(8,128)(2,1)S(1)}, bf16[64,192]{1,0:T(8,128)(2,1)S(1)}) custom-call(s32[128]{0:T(128)S(1)} %copy-done.2, bf16[4,64,192]{2,1,0:T(8,128)(2,1)S(1)} %get-tuple-element.13.q_in, bf16[4,64,192]{2,1,0:T(8,128)(2,1)S(1)} %get-tuple-element.12.g_in, bf16[64,384]{1,0:T(8,128)(2,1)S(1)} %copy-done, bf16[64,384]{1,0:T(8,128)(2,1)S(1)} %copy-done.1), custom_call_target="tpu_custom_call" | custom-call | tf_op jit(solution)/shard_map/pallas_call | solution.py:393
  71.3 0.8 %copy.10 = bf16[64,4,192]{2,1,0:T(4,128)(2,1)} copy(bf16[64,4,192]{2,0,1:T(8,128)(2,1)S(1)} %bitcast.5) | data formatting | bytes 196608
  72.1 0.7 fusion
Async XLA Ops:
  0.6 1.1 %copy-start.1 = (bf16[64,384]{1,0:T(8,128)(2,1)S(1)}, bf16[64,384]{1,0:T(8,128)(2,1)}, u32[]{:S(2)}) copy-start(bf16[64,384]{1,0:T(8,128)(2,1)} %v_in.1) | copy-start | bytes 147460
  0.6 1.1 %copy-start = (bf16[64,384]{1,0:T(8,128)(2,1)S(1)}, bf16[64,384]{1,0:T(8,128)(2,1)}, u32[]{:S(2)}) copy-start(bf16[64,384]{1,0:T(8,128)(2,1)} %k_in.1) | copy-start | bytes 147460
  1.7 0.7 copy-start.2

commit v5 on v4

--- a/solution.py
+++ b/solution.py
@@ -29,8 +29,8 @@
     stripe, q_in, g_in, k_in, v_in, dq_out, dkv_out,
     qg, kv, qga, kva, kvu, kt, wq, wg, prob, grad,
     tile_top, tile_sum, tile_mix, stat, stat_in, fac, delta,
-    dqt, dkf, own, sbs, sbr, l1s, relay, fin, dqb, dqr, l2s, l2r,
-    loc_sem, send_sem, recv_sem, l2_s, l2_r,
+    dqt, dkf, own, sbs, sbr, l1s, relay, fin, fwd, dks, dqb, dqr,
+    loc_sem, send_sem, recv_sem, f_s, f_r, r_s, r_r, w_r,
 ):
     b, y, t = lax.axis_index("blk"), lax.axis_index("uly"), lax.axis_index("tp")
     x, zl = b // 8, b % 8
@@ -77,12 +77,23 @@
 
     for to in peers:
         greet(to)
-    mine = (c == 0) & (y % 2 == 0) & (h == y // 2)
-    for hs in range(2):
-
-        @pl.when(jnp.logical_not(mine & (h == hs)))
-        def _():
-            greet(dev(x, t, hs * 8 + zl, ((t - y + 4) % 4) // 2))
+    home = y // 2
+    mine = (c == 0) & (y % 2 == 0) & (h == home)
+    near = (0, 1, 15, 2, 14, 3, 13)
+    straight = [((z + d) % 16) // 8 == home for d in near]
+    n_targets = 2
+    for flag in straight:
+        n_targets = n_targets + jnp.where(flag, 2, 0)
+    giver = ((t - y + 4) % 4) // 2
+    for d in near + (4, 12):
+        to = dev(x, t, (z + d) % 16, giver)
+        if d:
+            greet(to)
+        else:
+
+            @pl.when(jnp.logical_not(mine))
+            def _():
+                greet(to)
 
     for g in range(4):
         part = slice(g * HEAD, (g + 1) * HEAD)
@@ -93,7 +104,7 @@
         qg[g] = jnp.concatenate(
             [qs[:, :HEAD], gs[:, :HEAD], qs[:, HEAD:], gs[:, HEAD:]], axis=1
         )
-    pl.semaphore_wait(barrier, len(peers) + 2 - jnp.where(mine, 1, 0))
+    pl.semaphore_wait(barrier, len(peers) + n_targets - jnp.where(mine, 1, 0))
 
     half = pl.ds(pl.multiple_of(16 * c, 16), 16)
 
@@ -227,19 +238,30 @@
     got("s0", kva.at[1 - c, zl])
     unpack(0)
     tile(x, rows_of(x), zl, True)
-    for lo, count in ((1, 4), (5, 3)):
+
+    def take_keys(lo, count):
         for n in range(lo, lo + count):
             share_kv(n)
         for n in range(lo, lo + count):
             got(f"s{n}", kva.at[1 - c, order(n)])
             unpack(n)
-        tiles(x, lo, count)
-    for i in (1, 3, 2):
+
+    def take_rows(i):
         xs = (x - i + 4) % 4
         for j in range(4):
             got(f"x{i}_{j}", qga.at[xs, j])
         rows_in(xs)
-        tiles(xs, 0, 4, 2)
+        return xs
+
+    take_keys(1, 4)
+    tiles(x, 1, 4)
+    across = take_rows(2)
+    tiles(across, 0, 4)
+    take_keys(5, 3)
+    tiles(x, 5, 3)
+    tiles(across, 4, 4)
+    for i in (1, 3):
+        tiles(take_rows(i), 0, 4, 2)
 
     top = tile_top[0]
     for kc in range(1, 8):
@@ -279,26 +301,41 @@
     for kc in range(8):
         fac[kc] = jnp.exp2(tile_top[kc] - all_top) * inverse
 
-    steps = (zsteps[7], 3, 13, 2, 14, 1, 15, 0)
+    steps = near + (4,)
+    relays = (jnp.where(c == 0, 12, 4), 13, 3, 14, 2, 15, 1)
+    slots = (3, 2, 2, 1, 1, 0, 0)
+    guarded = []
+
+    def send_if(flag, src, dst, ss, rs, to):
+        copy = pltpu.make_async_remote_copy(
+            src_ref=src, dst_ref=dst, send_sem=ss, recv_sem=rs, device_id=to, device_id_type=MESH
+        )
+
+        @pl.when(flag)
+        def _():
+            copy.start()
+
+        guarded.append((flag, copy))
+
+    def owner(q, d):
+        return dev(x, (y - 2 * c - q + 4) % 4, (z + d) % 16, y % 2)
 
     def give(k):
         got(f"sb{k}", sbr.at[k])
-        total = own[k] + sbr[k].astype(F32)
-        if k in (3, 4):
-            got(f"r{k - 2}", relay.at[k - 2])
-            if k == 3:
-                got("r0", relay.at[0])
-            far = relay[0].astype(F32)
-            total = total + relay[k - 2].astype(F32)
-            total = total + jnp.where(c == k - 3, far, jnp.zeros_like(far))
-        l1s[k] = total.astype(BF16)
-        if k < 3:
-            send(f"r{k}", l1s.at[k], relay.at[k], on_z((jnp.where(c == 0, 2, 14), 1, 15)[k]))
-        else:
-            send(f"f{k}", l1s.at[k], fin.at[k - 3], on_z(steps[k]))
+        l1s[k] = (own[k] + sbr[k].astype(F32)).astype(BF16)
+        for q in range(2):
+            flag = straight[k]
+            if k == 0 and q == 0:
+                flag = flag & jnp.logical_not(mine)
+            send_if(flag, l1s.at[k, q], fin.at[k], f_s.at[k, q], f_r.at[k], owner(q, near[k]))
+        send_if(
+            jnp.logical_not(straight[k]), l1s.at[k], relay.at[slots[k]],
+            r_s.at[k], r_r.at[slots[k]], on_z(relays[k]),
+        )
 
     def packed(rows):
-        return jnp.concatenate([rows[:TOK], rows[TOK:]], axis=1)
+        rows = rows.reshape(2, TOK, WIDE)
+        return jnp.concatenate([rows[:, :32], rows[:, 32:]], axis=2)
 
     for k in range(8):
         kc = (zl + steps[k]) % 8
@@ -314,9 +351,10 @@
         sbs[k] = packed(dkf[pl.ds(pl.multiple_of(128 * (1 - c), 128), 128)]).astype(BF16)
         own[k] = packed(dkf[pl.ds(pl.multiple_of(128 * c, 128), 128)])
         send(f"sb{k}", sbs.at[k], sbr.at[k], sib)
-        if k in (2, 3, 4, 7):
+        if k >= 2:
             give(k - 2)
 
+    give(6)
     for i in (2, 1, 3, 0):
         xs = (x + i) % 4
         pair = dqt[pl.ds(xs * 2, 2)].reshape(WIDE, RT)
@@ -328,37 +366,33 @@
                     f"dq{i}_{j}", dqb.at[i, j], dqr.at[i, y],
                     dev(xs, (y - j + 4) % 4, z, c),
                 )
-        if i == 2:
-            give(6)
-        if i == 1:
-            give(3)
-            give(4)
     dqr[0, y] = dqb[0, 0]
 
     got("sb7", sbr.at[7])
     total = own[7] + sbr[7].astype(F32)
-    for k in range(3, 7):
-        got(f"f{k}", fin.at[k - 3])
-        total = total + fin[k - 3].astype(F32)
-    left = lax.broadcasted_iota(jnp.int32, (TOK, WIDE), 1) < HEAD
+    for k in range(3):
+        pltpu.make_async_copy(relay.at[k], relay.at[k], r_r.at[k]).wait()
+        total = total + relay[k].astype(F32)
+    ahead = ((z - 8 * home + 16 + 12) % 16) < 8
+    fourth = ahead == (c == 0)
+    dks[...] = total
+
+    @pl.when(fourth)
+    def _():
+        pltpu.make_async_copy(relay.at[3], relay.at[3], r_r.at[3]).wait()
+        dks[...] += relay[3].astype(F32)
+
+    l1s[7] = dks[...].astype(BF16)
+    side = jnp.where(ahead, 0, 1)
     for q in range(2):
-        l2s[q] = (total[:, q * WIDE : (q + 1) * WIDE] * jnp.where(left, SCALE, 1.0)).astype(BF16)
-    for q in range(2):
-        j = 2 * c + q
-        yo = (y - j + 4) % 4
-        is_self = mine & (yo == y)
-        copy = pltpu.make_async_remote_copy(
-            src_ref=l2s.at[q], dst_ref=l2r.at[h], send_sem=l2_s.at[q], recv_sem=l2_r.at[h],
-            device_id=dev(x, yo, 8 * (y // 2) + zl, y % 2), device_id_type=MESH,
-        )
-
-        @pl.when(jnp.logical_not(is_self))
-        def _():
-            copy.start()
-
-        @pl.when(is_self)
-        def _():
-            l2r[h] = l2s[q]
+        send_if(
+            c >= 0, l1s.at[7, q], fwd.at[side], f_s.at[7, q], w_r.at[side],
+            owner(q, jnp.where(ahead, 12, 4)),
+        )
+
+    @pl.when(mine)
+    def _():
+        fin[0] = l1s[0, 0]
 
     for j in range(4):
         gs = (y + j) % 4
@@ -370,21 +404,25 @@
         dq_out[gs, :32] = total[:, :WIDE].astype(BF16)
         dq_out[gs, 32:] = total[:, WIDE:].astype(BF16)
 
-    for hs in range(2):
-
-        @pl.when(jnp.logical_not(mine & (h == hs)))
-        def _():
-            pltpu.make_async_copy(l2r.at[hs], l2r.at[hs], l2_r.at[hs]).wait()
-
-    dkv_out[...] = (l2r[0].astype(F32) + l2r[1].astype(F32)).astype(BF16)
+    @pl.when(jnp.logical_not(mine))
+    def _():
+        pltpu.make_async_copy(fin.at[0], fin.at[0], f_r.at[0]).wait()
+
+    total = fin[0].astype(F32)
+    for k in range(1, 7):
+        pltpu.make_async_copy(fin.at[k], fin.at[k], f_r.at[k]).wait()
+        total = total + fin[k].astype(F32)
+    for side in range(2):
+        pltpu.make_async_copy(fwd.at[side], fwd.at[side], w_r.at[side]).wait()
+        total = total + fwd[side].astype(F32)
+    left = lax.broadcasted_iota(jnp.int32, (32, WIDE), 1) < HEAD
+    scale = jnp.where(left, SCALE, 1.0)
+    dkv_out[:32] = (total[:, :WIDE] * scale).astype(BF16)
+    dkv_out[32:] = (total[:, WIDE:] * scale).astype(BF16)
     for copy in sent:
         copy.wait_send()
-    for q in range(2):
-        yo = (y - 2 * c - q + 4) % 4
-
-        @pl.when(jnp.logical_not(mine & (yo == y)))
-        def _():
-            pltpu.make_async_copy(l2s.at[q], l2s.at[q], l2_s.at[q]).wait()
+    for flag, copy in guarded:
+        pl.when(flag)(copy.wait_send)
 
 
 def per_device(query_matrix, key_matrix, value_matrix, output_gradient, stripe_map):
@@ -418,17 +456,18 @@
             pltpu.VMEM((8, RT), F32),
             pltpu.VMEM((8, HEAD, RT), F32),
             pltpu.VMEM((RT, WIDE), F32),
-            pltpu.VMEM((8, TOK, 2 * WIDE), F32),
-            pltpu.VMEM((8, TOK, 2 * WIDE), BF16),
-            pltpu.VMEM((8, TOK, 2 * WIDE), BF16),
-            pltpu.VMEM((7, TOK, 2 * WIDE), BF16),
-            pltpu.VMEM((3, TOK, 2 * WIDE), BF16),
-            pltpu.VMEM((4, TOK, 2 * WIDE), BF16),
+            pltpu.VMEM((8, 2, 32, 2 * WIDE), F32),
+            pltpu.VMEM((8, 2, 32, 2 * WIDE), BF16),
+            pltpu.VMEM((8, 2, 32, 2 * WIDE), BF16),
+            pltpu.VMEM((8, 2, 32, 2 * WIDE), BF16),
+            pltpu.VMEM((4, 2, 32, 2 * WIDE), BF16),
+            pltpu.VMEM((7, 32, 2 * WIDE), BF16),
+            pltpu.VMEM((2, 32, 2 * WIDE), BF16),
+            pltpu.VMEM((2, 32, 2 * WIDE), F32),
             pltpu.VMEM((4, 4, 32, 2 * WIDE), BF16),
             pltpu.VMEM((4, 4, 32, 2 * WIDE), BF16),
-            pltpu.VMEM((2, TOK, WIDE), BF16),
-            pltpu.VMEM((2, TOK, WIDE), BF16),
-            dma((2,)), dma((N_SEM,)), dma((N_SEM,)), dma((2,)), dma((2,)),
+            dma((2,)), dma((N_SEM,)), dma((N_SEM,)),
+            dma((8, 2)), dma((7,)), dma((7,)), dma((4,)), dma((2,)),
         ],
         compiler_params=pltpu.CompilerParams(
             collective_id=0, has_side_effects=True, vmem_limit_bytes=50 * 2**20

time: 73.5 us -> 75.9 us (1.033)
  the two profiles are of different devices: /device:TPU:1 before, /device:TPU:65 now
where the time goes in v5:
time: 75.9 us; the launch traced here: 75.8 us
  Pallas kernels  72 us (95%)
  local copies, waits for them, and re-layouts  3.1 us (4%)
    pallas_call x1, Pallas kernels, per_device(): pl.pallas_call(kernel, out_shape=[jax.ShapeDtypeStruct((4, TOK, WIDE), BF...  72 us

profile of v5, /device:TPU:65, one launch (start us, length us, event | category | flops | bytes accessed | tf_op | source)
XLA Modules:
  0.0 75.8 jit_solution(14267672178475946733)
XLA Ops:
  0.6 0.0 copy-start.1
  0.6 0.0 copy-start
  0.7 1.0 %copy_bitcast_fusion = (bf16[4,64,192]{2,1,0:T(8,128)(2,1)S(1)}, bf16[4,64,192]{2,1,0:T(8,128)(2,1)S(1)}) fusion(bf16[64,4,192]{2,1,0:T(4,128)(2,1)} %param.8, bf16[64,4,192]{2,1,0:T(4,128)(2,1)} %param.5), kind=kLoop, calls=%fused_computation | loop fusion | bytes 393216 | tf_op jit(solution)/shard_map/transpose | solution.py:478
  1.7 0.0 copy-start.2
  1.7 0.0 copy-done.1
  1.7 0.0 copy-done
  1.7 0.6 copy-done.2
  2.3 72.0 %shard_map.76 = (bf16[4,64,192]{2,1,0:T(8,128)(2,1)S(1)}, bf16[64,192]{1,0:T(8,128)(2,1)S(1)}) custom-call(s32[128]{0:T(128)S(1)} %copy-done.2, bf16[4,64,192]{2,1,0:T(8,128)(2,1)S(1)} %get-tuple-element.13.q_in, bf16[4,64,192]{2,1,0:T(8,128)(2,1)S(1)} %get-tuple-element.12.g_in, bf16[64,384]{1,0:T(8,128)(2,1)S(1)} %copy-done, bf16[64,384]{1,0:T(8,128)(2,1)S(1)} %copy-done.1), custom_call_target="tpu_custom_call" | custom-call | tf_op jit(solution)/shard_map/pallas_call | solution.py:431
  74.3 0.8 %copy.10 = bf16[64,4,192]{2,1,0:T(4,128)(2,1)} copy(bf16[64,4,192]{2,0,1:T(8,128)(2,1)S(1)} %bitcast.5) | data formatting | bytes 196608
  75.1 0.7 fusion
Async XLA Ops:
  0.6 1.1 %copy-start.1 = (bf16[64,384]{1,0:T(8,128)(2,1)S(1)}, bf16[64,384]{1,0:T(8,128)(2,1)}, u32[]{:S(2)}) copy-start(bf16[64,384]{1,0:T(8,128)(2,1)} %v_in.1) | copy-start | bytes 147460
  0.6 1.1 %copy-start = (bf16[64,384]{1,0:T(8,128)(2,1)S(1)}, bf16[64,384]{1,0:T(8,128)(2,1)}, u32[]{:S(2)}) copy-start(bf16[64,384]{1,0:T(8,128)(2,1)} %k_in.1) | copy-start | bytes 147460
  1.7 0.7 copy-start.2

commit v6 on v5

--- a/solution.py
+++ b/solution.py
@@ -30,7 +30,7 @@
     qg, kv, qga, kva, kvu, kt, wq, wg, prob, grad,
     tile_top, tile_sum, tile_mix, stat, stat_in, fac, delta,
     dqt, dkf, own, sbs, sbr, l1s, relay, fin, fwd, dks, dqb, dqr,
-    loc_sem, send_sem, recv_sem, f_s, f_r, r_s, r_r, w_r,
+    loc_sem, send_sem, recv_sem, f_s, f_r, r_s, r_r, w_r, sb_s, sb_r, dq_s, dq_r,
 ):
     b, y, t = lax.axis_index("blk"), lax.axis_index("uly"), lax.axis_index("tp")
     x, zl = b // 8, b % 8
@@ -54,14 +54,15 @@
     sent = []
     names = {}
 
-    def send(name, src, dst, to):
+    def send(name, src, dst, to, keep=True):
         n = names.setdefault(name, len(names))
         copy = pltpu.make_async_remote_copy(
             src_ref=src, dst_ref=dst, send_sem=send_sem.at[n], recv_sem=recv_sem.at[n],
             device_id=to, device_id_type=MESH,
         )
         copy.start()
-        sent.append(copy)
+        if keep:
+            sent.append(copy)
 
     def got(name, ref):
         pltpu.make_async_copy(ref, ref, recv_sem.at[names[name]]).wait()
@@ -148,7 +149,7 @@
         if n == 0:
             for d in range(1, 5):
                 send(f"k{d}_r", kva.at[c, zl, rest], kva.at[c, zl, rest], on_z(zsteps[d]))
-        send(f"s{n}", kva.at[c, zs], kva.at[c, zs], sib)
+        send(f"s{n}", kva.at[c, zs], kva.at[c, zs], sib, False)
 
     loc_kv.wait()
     share_kv(0)
@@ -223,45 +224,60 @@
             tile_sum[kc, pl.ds(rt, 1)] = jnp.sum(total, axis=0, keepdims=True)
             tile_mix[kc, pl.ds(rt, 1)] = jnp.sum(mixed, axis=0, keepdims=True)
 
-    def tiles(xs, lo, count, turns=1):
-        row_block = rows_of(xs)
-
-        def step(turn, _):
-            for n in range(count):
-                tile(xs, row_block, order(lo + turn * count + n))
-            return 0
-
-        lax.fori_loop(0, turns, step, 0)
-
     loc_qg.wait()
     rows_in(x)
     got("s0", kva.at[1 - c, zl])
-    unpack(0)
-    tile(x, rows_of(x), zl, True)
-
-    def take_keys(lo, count):
-        for n in range(lo, lo + count):
+
+    def unpacks(lo, hi):
+        def step(n, _):
+            unpack(n)
+            return 0
+
+        lax.fori_loop(lo, hi, step, 0)
+
+    def take_keys(lo, hi):
+        for n in range(lo, hi):
             share_kv(n)
-        for n in range(lo, lo + count):
+        for n in range(lo, hi):
             got(f"s{n}", kva.at[1 - c, order(n)])
-            unpack(n)
 
     def take_rows(i):
         xs = (x - i + 4) % 4
         for j in range(4):
             got(f"x{i}_{j}", qga.at[xs, j])
         rows_in(xs)
-        return xs
 
     take_keys(1, 4)
-    tiles(x, 1, 4)
-    across = take_rows(2)
-    tiles(across, 0, 4)
-    take_keys(5, 3)
-    tiles(x, 5, 3)
-    tiles(across, 4, 4)
-    for i in (1, 3):
-        tiles(take_rows(i), 0, 4, 2)
+    unpacks(0, 4)
+
+    def quad(n, _):
+        xs = (x + jnp.where(n < 4, 2 * (n % 2), jnp.where(n < 6, 3, 1))) % 4
+        lo = 4 * jnp.where(n < 4, n // 2, n % 2)
+
+        @pl.when(n == 1)
+        def _():
+            tile(x, rows_of(x), zl, True)
+            take_rows(2)
+
+        @pl.when(n == 2)
+        def _():
+            take_keys(4, 8)
+            unpacks(4, 8)
+
+        @pl.when(n == 4)
+        def _():
+            take_rows(1)
+
+        @pl.when(n == 6)
+        def _():
+            take_rows(3)
+
+        row_block = rows_of(xs)
+        for m in range(4):
+            tile(xs, row_block, order(lo + m))
+        return 0
+
+    lax.fori_loop(0, 8, quad, 0)
 
     top = tile_top[0]
     for kc in range(1, 8):
@@ -301,44 +317,57 @@
     for kc in range(8):
         fac[kc] = jnp.exp2(tile_top[kc] - all_top) * inverse
 
-    steps = near + (4,)
-    relays = (jnp.where(c == 0, 12, 4), 13, 3, 14, 2, 15, 1)
-    slots = (3, 2, 2, 1, 1, 0, 0)
-    guarded = []
-
-    def send_if(flag, src, dst, ss, rs, to):
-        copy = pltpu.make_async_remote_copy(
-            src_ref=src, dst_ref=dst, send_sem=ss, recv_sem=rs, device_id=to, device_id_type=MESH
-        )
-
-        @pl.when(flag)
-        def _():
-            copy.start()
-
-        guarded.append((flag, copy))
+    def step_of(k):
+        return jnp.where(k % 2 == 1, (k + 1) // 2, (16 - k // 2) % 16)
 
     def owner(q, d):
         return dev(x, (y - 2 * c - q + 4) % 4, (z + d) % 16, y % 2)
 
+    def ways(k):
+        d = step_of(k)
+        rho = jnp.where(k == 0, jnp.where(c == 0, 12, 4), (d + jnp.where(k % 2 == 1, 12, 4)) % 16)
+        slot = jnp.where(k == 0, 3, 3 - (k + 1) // 2)
+        flag = ((z + d) % 16) // 8 == home
+        copies = []
+        for q in range(2):
+            copies.append(
+                (
+                    flag & jnp.logical_not(mine & (k == 0)) if q == 0 else flag,
+                    pltpu.make_async_remote_copy(
+                        src_ref=l1s.at[k, q], dst_ref=fin.at[k], send_sem=f_s.at[k, q],
+                        recv_sem=f_r.at[k], device_id=owner(q, d), device_id_type=MESH,
+                    ),
+                )
+            )
+        copies.append(
+            (
+                jnp.logical_not(flag),
+                pltpu.make_async_remote_copy(
+                    src_ref=l1s.at[k], dst_ref=relay.at[slot], send_sem=r_s.at[k],
+                    recv_sem=r_r.at[slot], device_id=on_z(rho), device_id_type=MESH,
+                ),
+            )
+        )
+        return copies
+
     def give(k):
-        got(f"sb{k}", sbr.at[k])
+        pltpu.make_async_copy(sbr.at[k], sbr.at[k], sb_r.at[k]).wait()
         l1s[k] = (own[k] + sbr[k].astype(F32)).astype(BF16)
-        for q in range(2):
-            flag = straight[k]
-            if k == 0 and q == 0:
-                flag = flag & jnp.logical_not(mine)
-            send_if(flag, l1s.at[k, q], fin.at[k], f_s.at[k, q], f_r.at[k], owner(q, near[k]))
-        send_if(
-            jnp.logical_not(straight[k]), l1s.at[k], relay.at[slots[k]],
-            r_s.at[k], r_r.at[slots[k]], on_z(relays[k]),
+        for flag, copy in ways(k):
+            pl.when(flag)(copy.start)
+
+    def share(k):
+        return pltpu.make_async_remote_copy(
+            src_ref=sbs.at[k], dst_ref=sbr.at[k], send_sem=sb_s.at[k], recv_sem=sb_r.at[k],
+            device_id=sib, device_id_type=MESH,
         )
 
     def packed(rows):
         rows = rows.reshape(2, TOK, WIDE)
         return jnp.concatenate([rows[:, :32], rows[:, 32:]], axis=2)
 
-    for k in range(8):
-        kc = (zl + steps[k]) % 8
+    def key_group(k, _):
+        kc = (zl + step_of(k)) % 8
 
         def rows_step(rt, dkv):
             p = prob[rt, kc] * fac[kc, pl.ds(rt, 1)]
@@ -350,25 +379,38 @@
         dkf[...] = lax.fori_loop(0, 8, rows_step, jnp.zeros((RT, WIDE), F32), unroll=8)
         sbs[k] = packed(dkf[pl.ds(pl.multiple_of(128 * (1 - c), 128), 128)]).astype(BF16)
         own[k] = packed(dkf[pl.ds(pl.multiple_of(128 * c, 128), 128)])
-        send(f"sb{k}", sbs.at[k], sbr.at[k], sib)
-        if k >= 2:
+        share(k).start()
+
+        @pl.when(k >= 2)
+        def _():
             give(k - 2)
 
+        return 0
+
+    lax.fori_loop(0, 8, key_group, 0)
     give(6)
-    for i in (2, 1, 3, 0):
-        xs = (x + i) % 4
-        pair = dqt[pl.ds(xs * 2, 2)].reshape(WIDE, RT)
+
+    def row_ways(i, j):
+        return pltpu.make_async_remote_copy(
+            src_ref=dqb.at[i, j], dst_ref=dqr.at[i, y], send_sem=dq_s.at[i, j],
+            recv_sem=dq_r.at[i, j],
+            device_id=dev((x + i) % 4, (y - j + 4) % 4, z, c), device_id_type=MESH,
+        )
+
+    def rows_out(n, _):
+        i = jnp.where(n == 0, 2, jnp.where(n == 1, 1, jnp.where(n == 2, 3, 0)))
+        pair = dqt[pl.ds(((x + i) % 4) * 2, 2)].reshape(WIDE, RT)
         rows = (jnp.transpose(pair) * SCALE).reshape(4, TOK, WIDE)
         dqb[i] = jnp.concatenate([rows[:, :32], rows[:, 32:]], axis=2).astype(BF16)
-        for j in (2, 1, 3, 0):
-            if i or j:
-                send(
-                    f"dq{i}_{j}", dqb.at[i, j], dqr.at[i, y],
-                    dev(xs, (y - j + 4) % 4, z, c),
-                )
+        for j in (2, 1, 3):
+            row_ways(i, j).start()
+        pl.when(i > 0)(row_ways(i, 0).start)
+        return 0
+
+    lax.fori_loop(0, 4, rows_out, 0)
     dqr[0, y] = dqb[0, 0]
 
-    got("sb7", sbr.at[7])
+    pltpu.make_async_copy(sbr.at[7], sbr.at[7], sb_r.at[7]).wait()
     total = own[7] + sbr[7].astype(F32)
     for k in range(3):
         pltpu.make_async_copy(relay.at[k], relay.at[k], r_r.at[k]).wait()
@@ -384,25 +426,38 @@
 
     l1s[7] = dks[...].astype(BF16)
     side = jnp.where(ahead, 0, 1)
-    for q in range(2):
-        send_if(
-            c >= 0, l1s.at[7, q], fwd.at[side], f_s.at[7, q], w_r.at[side],
-            owner(q, jnp.where(ahead, 12, 4)),
-        )
+    forward = [
+        pltpu.make_async_remote_copy(
+            src_ref=l1s.at[7, q], dst_ref=fwd.at[side], send_sem=f_s.at[7, q],
+            recv_sem=w_r.at[side], device_id=owner(q, jnp.where(ahead, 12, 4)),
+            device_id_type=MESH,
+        )
+        for q in range(2)
+    ]
+    for copy in forward:
+        copy.start()
 
     @pl.when(mine)
     def _():
         fin[0] = l1s[0, 0]
 
-    for j in range(4):
+    def rows_sum(j, _):
         gs = (y + j) % 4
-        total = jnp.zeros((32, 2 * WIDE), F32)
-        for i in (0, 1, 3, 2):
-            if i or j:
-                got(f"dq{i}_{j}", dqr.at[i, gs])
+
+        @pl.when(j > 0)
+        def _():
+            pltpu.make_async_copy(dqr.at[0, gs], dqr.at[0, gs], dq_r.at[0, j]).wait()
+
+        for i in (1, 3, 2):
+            pltpu.make_async_copy(dqr.at[i, gs], dqr.at[i, gs], dq_r.at[i, j]).wait()
+        total = dqr[0, gs].astype(F32)
+        for i in range(1, 4):
             total = total + dqr[i, gs].astype(F32)
         dq_out[gs, :32] = total[:, :WIDE].astype(BF16)
         dq_out[gs, 32:] = total[:, WIDE:].astype(BF16)
+        return 0
+
+    lax.fori_loop(0, 4, rows_sum, 0)
 
     @pl.when(jnp.logical_not(mine))
     def _():
@@ -421,8 +476,30 @@
     dkv_out[32:] = (total[:, WIDE:] * scale).astype(BF16)
     for copy in sent:
         copy.wait_send()
-    for flag, copy in guarded:
-        pl.when(flag)(copy.wait_send)
+    for copy in forward:
+        copy.wait_send()
+    for n in range(8):
+        pltpu.make_async_copy(kva.at[0, 0], kva.at[0, 0], send_sem.at[names[f"s{n}"]]).wait()
+
+    def ended(k, _):
+        share(k).wait_send()
+
+        @pl.when(k < 7)
+        def _():
+            for flag, copy in ways(k):
+                pl.when(flag)(copy.wait_send)
+
+        return 0
+
+    lax.fori_loop(0, 8, ended, 0)
+
+    def rows_ended(i, _):
+        for j in range(1, 4):
+            row_ways(i, j).wait_send()
+        pl.when(i > 0)(row_ways(i, 0).wait_send)
+        return 0
+
+    lax.fori_loop(0, 4, rows_ended, 0)
 
 
 def per_device(query_matrix, key_matrix, value_matrix, output_gradient, stripe_map):
@@ -468,6 +545,7 @@
             pltpu.VMEM((4, 4, 32, 2 * WIDE), BF16),
             dma((2,)), dma((N_SEM,)), dma((N_SEM,)),
             dma((8, 2)), dma((7,)), dma((7,)), dma((4,)), dma((2,)),
+            dma((8,)), dma((8,)), dma((4, 4)), dma((4, 4)),
         ],
         compiler_params=pltpu.CompilerParams(
             collective_id=0, has_side_effects=True, vmem_limit_bytes=50 * 2**20

time: 75.9 us -> 77.9 us (1.026)
  Pallas kernels: 72 us -> 73.9 us
    pallas_call x1, Pallas kernels: 72 us -> 73.9 us  [per_device(): pl.pallas_call(kernel, out_shape=[jax.ShapeDtypeStruct((4, TOK, WIDE), BF...]
where the time goes in v6:
time: 77.9 us; the launch traced here: 77.7 us
  Pallas kernels  73.9 us (95%)
  local copies, waits for them, and re-layouts  3.1 us (4%)
    pallas_call x1, Pallas kernels, per_device(): pl.pallas_call(kernel, out_shape=[jax.ShapeDtypeStruct((4, TOK, WIDE), BF...  73.9 us

profile of v6, /device:TPU:65, one launch (start us, length us, event | category | flops | bytes accessed | tf_op | source)
XLA Modules:
  0.0 77.7 jit_solution(15744499495393033317)
XLA Ops:
  0.6 0.0 copy-start.1
  0.6 0.0 copy-start
  0.7 1.0 %copy_bitcast_fusion = (bf16[4,64,192]{2,1,0:T(8,128)(2,1)S(1)}, bf16[4,64,192]{2,1,0:T(8,128)(2,1)S(1)}) fusion(bf16[64,4,192]{2,1,0:T(4,128)(2,1)} %param.8, bf16[64,4,192]{2,1,0:T(4,128)(2,1)} %param.5), kind=kLoop, calls=%fused_computation | loop fusion | bytes 393216 | tf_op jit(solution)/shard_map/transpose | solution.py:556
  1.7 0.0 copy-start.2
  1.7 0.0 copy-done.1
  1.7 0.0 copy-done
  1.7 0.6 copy-done.2
  2.3 73.9 %shard_map.76 = (bf16[4,64,192]{2,1,0:T(8,128)(2,1)S(1)}, bf16[64,192]{1,0:T(8,128)(2,1)S(1)}) custom-call(s32[128]{0:T(128)S(1)} %copy-done.2, bf16[4,64,192]{2,1,0:T(8,128)(2,1)S(1)} %get-tuple-element.13.q_in, bf16[4,64,192]{2,1,0:T(8,128)(2,1)S(1)} %get-tuple-element.12.g_in, bf16[64,384]{1,0:T(8,128)(2,1)S(1)} %copy-done, bf16[64,384]{1,0:T(8,128)(2,1)S(1)} %copy-done.1), custom_call_target="tpu_custom_call" | custom-call | tf_op jit(solution)/shard_map/pallas_call | solution.py:508
  76.3 0.8 copy.10
  77.0 0.7 fusion
Async XLA Ops:
  0.6 1.1 %copy-start.1 = (bf16[64,384]{1,0:T(8,128)(2,1)S(1)}, bf16[64,384]{1,0:T(8,128)(2,1)}, u32[]{:S(2)}) copy-start(bf16[64,384]{1,0:T(8,128)(2,1)} %v_in.1) | copy-start | bytes 147460
  0.6 1.1 %copy-start = (bf16[64,384]{1,0:T(8,128)(2,1)S(1)}, bf16[64,384]{1,0:T(8,128)(2,1)}, u32[]{:S(2)}) copy-start(bf16[64,384]{1,0:T(8,128)(2,1)} %k_in.1) | copy-start | bytes 147460
  1.7 0.7 copy-start.2

commit v7 on v5

--- a/solution.py
+++ b/solution.py
@@ -29,8 +29,8 @@
     stripe, q_in, g_in, k_in, v_in, dq_out, dkv_out,
     qg, kv, qga, kva, kvu, kt, wq, wg, prob, grad,
     tile_top, tile_sum, tile_mix, stat, stat_in, fac, delta,
-    dqt, dkf, own, sbs, sbr, l1s, relay, fin, fwd, dks, dqb, dqr,
-    loc_sem, send_sem, recv_sem, f_s, f_r, r_s, r_r, w_r,
+    dqt, dkf, own, sbs, sbr, l1s, land, l2s, fin, dqb, dqr,
+    loc_sem, send_sem, recv_sem, f_s, f_r, l_s, l_r, sb_s, sb_r, dq_s, dq_r,
 ):
     b, y, t = lax.axis_index("blk"), lax.axis_index("uly"), lax.axis_index("tp")
     x, zl = b // 8, b % 8
@@ -79,21 +79,11 @@
         greet(to)
     home = y // 2
     mine = (c == 0) & (y % 2 == 0) & (h == home)
-    near = (0, 1, 15, 2, 14, 3, 13)
-    straight = [((z + d) % 16) // 8 == home for d in near]
-    n_targets = 2
-    for flag in straight:
-        n_targets = n_targets + jnp.where(flag, 2, 0)
-    giver = ((t - y + 4) % 4) // 2
-    for d in near + (4, 12):
-        to = dev(x, t, (z + d) % 16, giver)
-        if d:
-            greet(to)
-        else:
-
-            @pl.when(jnp.logical_not(mine))
-            def _():
-                greet(to)
+    for hs in range(2):
+
+        @pl.when(jnp.logical_not(mine & (h == hs)))
+        def _():
+            greet(dev(x, t, hs * 8 + zl, ((t - y + 4) % 4) // 2))
 
     for g in range(4):
         part = slice(g * HEAD, (g + 1) * HEAD)
@@ -104,7 +94,7 @@
         qg[g] = jnp.concatenate(
             [qs[:, :HEAD], gs[:, :HEAD], qs[:, HEAD:], gs[:, HEAD:]], axis=1
         )
-    pl.semaphore_wait(barrier, len(peers) + n_targets - jnp.where(mine, 1, 0))
+    pl.semaphore_wait(barrier, len(peers) + 2 - jnp.where(mine, 1, 0))
 
     half = pl.ds(pl.multiple_of(16 * c, 16), 16)
 
@@ -301,44 +291,37 @@
     for kc in range(8):
         fac[kc] = jnp.exp2(tile_top[kc] - all_top) * inverse
 
-    steps = near + (4,)
-    relays = (jnp.where(c == 0, 12, 4), 13, 3, 14, 2, 15, 1)
-    slots = (3, 2, 2, 1, 1, 0, 0)
-    guarded = []
-
-    def send_if(flag, src, dst, ss, rs, to):
-        copy = pltpu.make_async_remote_copy(
-            src_ref=src, dst_ref=dst, send_sem=ss, recv_sem=rs, device_id=to, device_id_type=MESH
-        )
-
-        @pl.when(flag)
-        def _():
-            copy.start()
-
-        guarded.append((flag, copy))
-
-    def owner(q, d):
-        return dev(x, (y - 2 * c - q + 4) % 4, (z + d) % 16, y % 2)
+    def step_of(k):
+        return jnp.where(k % 2 == 1, (7 - k) // 2, 4 + k // 2)
 
     def give(k):
-        got(f"sb{k}", sbr.at[k])
-        l1s[k] = (own[k] + sbr[k].astype(F32)).astype(BF16)
-        for q in range(2):
-            flag = straight[k]
-            if k == 0 and q == 0:
-                flag = flag & jnp.logical_not(mine)
-            send_if(flag, l1s.at[k, q], fin.at[k], f_s.at[k, q], f_r.at[k], owner(q, near[k]))
-        send_if(
-            jnp.logical_not(straight[k]), l1s.at[k], relay.at[slots[k]],
-            r_s.at[k], r_r.at[slots[k]], on_z(relays[k]),
+        d = jnp.where(k == 0, jnp.where(c == 0, 2, 14), 0)
+        d = jnp.where((k == 1) | (k == 5), 1, jnp.where((k == 2) | (k == 6), 15, d))
+        d = jnp.where(k == 3, 2, jnp.where(k == 4, 14, d))
+        return pltpu.make_async_remote_copy(
+            src_ref=l1s.at[k], dst_ref=land.at[k], send_sem=l_s.at[k], recv_sem=l_r.at[k],
+            device_id=on_z(d), device_id_type=MESH,
+        )
+
+    def landed(k):
+        pltpu.make_async_copy(land.at[k], land.at[k], l_r.at[k]).wait()
+
+    def both(k):
+        pltpu.make_async_copy(sbr.at[k], sbr.at[k], sb_r.at[k]).wait()
+        return own[k] + sbr[k].astype(F32)
+
+    def share(k):
+        return pltpu.make_async_remote_copy(
+            src_ref=sbs.at[k], dst_ref=sbr.at[k], send_sem=sb_s.at[k], recv_sem=sb_r.at[k],
+            device_id=sib, device_id_type=MESH,
         )
 
     def packed(rows):
         rows = rows.reshape(2, TOK, WIDE)
         return jnp.concatenate([rows[:, :32], rows[:, 32:]], axis=2)
 
-    for k in range(8):
-        kc = (zl + steps[k]) % 8
+    def key_group(k, _):
+        kc = (zl + step_of(k)) % 8
 
         def rows_step(rt, dkv):
             p = prob[rt, kc] * fac[kc, pl.ds(rt, 1)]
@@ -350,79 +333,115 @@
         dkf[...] = lax.fori_loop(0, 8, rows_step, jnp.zeros((RT, WIDE), F32), unroll=8)
         sbs[k] = packed(dkf[pl.ds(pl.multiple_of(128 * (1 - c), 128), 128)]).astype(BF16)
         own[k] = packed(dkf[pl.ds(pl.multiple_of(128 * c, 128), 128)])
-        send(f"sb{k}", sbs.at[k], sbr.at[k], sib)
-        if k >= 2:
-            give(k - 2)
-
-    give(6)
-    for i in (2, 1, 3, 0):
-        xs = (x + i) % 4
-        pair = dqt[pl.ds(xs * 2, 2)].reshape(WIDE, RT)
+        share(k).start()
+
+        @pl.when((k >= 2) & ((k < 5) | (k == 7)))
+        def _():
+            l1s[k - 2] = both(k - 2).astype(BF16)
+            give(k - 2).start()
+
+        return 0
+
+    lax.fori_loop(0, 8, key_group, 0)
+    l1s[6] = both(6).astype(BF16)
+    give(6).start()
+    landed(0)
+    for k in (3, 4):
+        landed(k - 2)
+        far = land[0].astype(F32)
+        total = both(k) + land[k - 2].astype(F32)
+        l1s[k] = (total + jnp.where(c == k - 3, far, jnp.zeros_like(far))).astype(BF16)
+        give(k).start()
+
+    def row_ways(i, j):
+        return pltpu.make_async_remote_copy(
+            src_ref=dqb.at[i, j], dst_ref=dqr.at[i, y], send_sem=dq_s.at[i, j],
+            recv_sem=dq_r.at[i, j],
+            device_id=dev((x + i) % 4, (y - j + 4) % 4, z, c), device_id_type=MESH,
+        )
+
+    def rows_out(n, _):
+        i = jnp.where(n == 0, 2, jnp.where(n == 1, 1, jnp.where(n == 2, 3, 0)))
+        pair = dqt[pl.ds(((x + i) % 4) * 2, 2)].reshape(WIDE, RT)
         rows = (jnp.transpose(pair) * SCALE).reshape(4, TOK, WIDE)
         dqb[i] = jnp.concatenate([rows[:, :32], rows[:, 32:]], axis=2).astype(BF16)
-        for j in (2, 1, 3, 0):
-            if i or j:
-                send(
-                    f"dq{i}_{j}", dqb.at[i, j], dqr.at[i, y],
-                    dev(xs, (y - j + 4) % 4, z, c),
-                )
+        for j in (2, 1, 3):
+            row_ways(i, j).start()
+        pl.when(i > 0)(row_ways(i, 0).start)
+        return 0
+
+    lax.fori_loop(0, 4, rows_out, 0)
     dqr[0, y] = dqb[0, 0]
 
-    got("sb7", sbr.at[7])
-    total = own[7] + sbr[7].astype(F32)
-    for k in range(3):
-        pltpu.make_async_copy(relay.at[k], relay.at[k], r_r.at[k]).wait()
-        total = total + relay[k].astype(F32)
-    ahead = ((z - 8 * home + 16 + 12) % 16) < 8
-    fourth = ahead == (c == 0)
-    dks[...] = total
-
-    @pl.when(fourth)
-    def _():
-        pltpu.make_async_copy(relay.at[3], relay.at[3], r_r.at[3]).wait()
-        dks[...] += relay[3].astype(F32)
-
-    l1s[7] = dks[...].astype(BF16)
-    side = jnp.where(ahead, 0, 1)
+    total = both(7)
+    for k in (5, 6, 3, 4):
+        landed(k)
+        total = total + land[k].astype(F32)
+    l2s[...] = total.astype(BF16)
+    forward = []
     for q in range(2):
-        send_if(
-            c >= 0, l1s.at[7, q], fwd.at[side], f_s.at[7, q], w_r.at[side],
-            owner(q, jnp.where(ahead, 12, 4)),
-        )
+        copy = pltpu.make_async_remote_copy(
+            src_ref=l2s.at[q], dst_ref=fin.at[h], send_sem=f_s.at[q], recv_sem=f_r.at[h],
+            device_id=dev(x, (y - 2 * c - q + 4) % 4, 8 * home + zl, y % 2), device_id_type=MESH,
+        )
+        if q:
+            copy.start()
+        else:
+            pl.when(jnp.logical_not(mine))(copy.start)
+        forward.append(copy)
 
     @pl.when(mine)
     def _():
-        fin[0] = l1s[0, 0]
-
-    for j in range(4):
+        fin[h] = l2s[0]
+
+    def rows_sum(j, _):
         gs = (y + j) % 4
-        total = jnp.zeros((32, 2 * WIDE), F32)
-        for i in (0, 1, 3, 2):
-            if i or j:
-                got(f"dq{i}_{j}", dqr.at[i, gs])
+
+        @pl.when(j > 0)
+        def _():
+            pltpu.make_async_copy(dqr.at[0, gs], dqr.at[0, gs], dq_r.at[0, j]).wait()
+
+        for i in (1, 3, 2):
+            pltpu.make_async_copy(dqr.at[i, gs], dqr.at[i, gs], dq_r.at[i, j]).wait()
+        total = dqr[0, gs].astype(F32)
+        for i in range(1, 4):
             total = total + dqr[i, gs].astype(F32)
         dq_out[gs, :32] = total[:, :WIDE].astype(BF16)
         dq_out[gs, 32:] = total[:, WIDE:].astype(BF16)
-
-    @pl.when(jnp.logical_not(mine))
-    def _():
-        pltpu.make_async_copy(fin.at[0], fin.at[0], f_r.at[0]).wait()
-
-    total = fin[0].astype(F32)
-    for k in range(1, 7):
-        pltpu.make_async_copy(fin.at[k], fin.at[k], f_r.at[k]).wait()
-        total = total + fin[k].astype(F32)
-    for side in range(2):
-        pltpu.make_async_copy(fwd.at[side], fwd.at[side], w_r.at[side]).wait()
-        total = total + fwd[side].astype(F32)
+        return 0
+
+    lax.fori_loop(0, 4, rows_sum, 0)
+
+    for hs in range(2):
+
+        @pl.when(jnp.logical_not(mine & (h == hs)))
+        def _():
+            pltpu.make_async_copy(fin.at[hs], fin.at[hs], f_r.at[hs]).wait()
+
+    total = fin[0].astype(F32) + fin[1].astype(F32)
     left = lax.broadcasted_iota(jnp.int32, (32, WIDE), 1) < HEAD
     scale = jnp.where(left, SCALE, 1.0)
     dkv_out[:32] = (total[:, :WIDE] * scale).astype(BF16)
     dkv_out[32:] = (total[:, WIDE:] * scale).astype(BF16)
     for copy in sent:
         copy.wait_send()
-    for flag, copy in guarded:
-        pl.when(flag)(copy.wait_send)
+    forward[1].wait_send()
+    pl.when(jnp.logical_not(mine))(forward[0].wait_send)
+    def ended(k, _):
+        share(k).wait_send()
+
+        pl.when(k < 7)(give(jnp.minimum(k, 6)).wait_send)
+        return 0
+
+    lax.fori_loop(0, 8, ended, 0)
+
+    def rows_ended(i, _):
+        for j in range(1, 4):
+            row_ways(i, j).wait_send()
+        pl.when(i > 0)(row_ways(i, 0).wait_send)
+        return 0
+
+    lax.fori_loop(0, 4, rows_ended, 0)
 
 
 def per_device(query_matrix, key_matrix, value_matrix, output_gradient, stripe_map):
@@ -459,15 +478,15 @@
             pltpu.VMEM((8, 2, 32, 2 * WIDE), F32),
             pltpu.VMEM((8, 2, 32, 2 * WIDE), BF16),
             pltpu.VMEM((8, 2, 32, 2 * WIDE), BF16),
-            pltpu.VMEM((8, 2, 32, 2 * WIDE), BF16),
-            pltpu.VMEM((4, 2, 32, 2 * WIDE), BF16),
-            pltpu.VMEM((7, 32, 2 * WIDE), BF16),
+            pltpu.VMEM((7, 2, 32, 2 * WIDE), BF16),
+            pltpu.VMEM((7, 2, 32, 2 * WIDE), BF16),
             pltpu.VMEM((2, 32, 2 * WIDE), BF16),
-            pltpu.VMEM((2, 32, 2 * WIDE), F32),
+            pltpu.VMEM((2, 32, 2 * WIDE), BF16),
             pltpu.VMEM((4, 4, 32, 2 * WIDE), BF16),
             pltpu.VMEM((4, 4, 32, 2 * WIDE), BF16),
             dma((2,)), dma((N_SEM,)), dma((N_SEM,)),
-            dma((8, 2)), dma((7,)), dma((7,)), dma((4,)), dma((2,)),
+            dma((2,)), dma((2,)), dma((7,)), dma((7,)),
+            dma((8,)), dma((8,)), dma((4, 4)), dma((4, 4)),
         ],
         compiler_params=pltpu.CompilerParams(
             collective_id=0, has_side_effects=True, vmem_limit_bytes=50 * 2**20

time: 75.9 us -> 69.8 us (0.920)
  the two profiles are of different devices: /device:TPU:65 before, /device:TPU:1 now
where the time goes in v7:
time: 69.8 us; the launch traced here: 69.5 us
  Pallas kernels  65.7 us (94%)
  local copies, waits for them, and re-layouts  3.1 us (4%)
    pallas_call x1, Pallas kernels, per_device(): pl.pallas_call(kernel, out_shape=[jax.ShapeDtypeStruct((4, TOK, WIDE), BF...  65.7 us
    unnamed x7, local copies, waits for them, and re-layouts  1.4 us

profile of v7, /device:TPU:1, one launch (start us, length us, event | category | flops | bytes accessed | tf_op | source)
XLA Modules:
  0.0 69.5 jit_solution(12240564003058609500)
XLA Ops:
  0.6 0.0 copy-start.1
  0.6 0.0 copy-start
  0.7 1.0 %copy_bitcast_fusion = (bf16[4,64,192]{2,1,0:T(8,128)(2,1)S(1)}, bf16[4,64,192]{2,1,0:T(8,128)(2,1)S(1)}) fusion(bf16[64,4,192]{2,1,0:T(4,128)(2,1)} %param.8, bf16[64,4,192]{2,1,0:T(4,128)(2,1)} %param.5), kind=kLoop, calls=%fused_computation | loop fusion | bytes 393216 | tf_op jit(solution)/shard_map/transpose | solution.py:497
  1.7 0.0 copy-start.2
  1.7 0.0 copy-done.1
  1.7 0.0 copy-done
  1.7 0.6 copy-done.2
  2.3 65.7 %shard_map.76 = (bf16[4,64,192]{2,1,0:T(8,128)(2,1)S(1)}, bf16[64,192]{1,0:T(8,128)(2,1)S(1)}) custom-call(s32[128]{0:T(128)S(1)} %copy-done.2, bf16[4,64,192]{2,1,0:T(8,128)(2,1)S(1)} %get-tuple-element.13.q_in, bf16[4,64,192]{2,1,0:T(8,128)(2,1)S(1)} %get-tuple-element.12.g_in, bf16[64,384]{1,0:T(8,128)(2,1)S(1)} %copy-done, bf16[64,384]{1,0:T(8,128)(2,1)S(1)} %copy-done.1), custom_call_target="tpu_custom_call" | custom-call | tf_op jit(solution)/shard_map/pallas_call | solution.py:450
  68.0 0.8 %copy.10 = bf16[64,4,192]{2,1,0:T(4,128)(2,1)} copy(bf16[64,4,192]{2,0,1:T(8,128)(2,1)S(1)} %bitcast.5) | data formatting | bytes 196608
  68.8 0.7 fusion
Async XLA Ops:
  0.6 1.1 %copy-start.1 = (bf16[64,384]{1,0:T(8,128)(2,1)S(1)}, bf16[64,384]{1,0:T(8,128)(2,1)}, u32[]{:S(2)}) copy-start(bf16[64,384]{1,0:T(8,128)(2,1)} %v_in.1) | copy-start | bytes 147460
  0.6 1.1 %copy-start = (bf16[64,384]{1,0:T(8,128)(2,1)S(1)}, bf16[64,384]{1,0:T(8,128)(2,1)}, u32[]{:S(2)}) copy-start(bf16[64,384]{1,0:T(8,128)(2,1)} %k_in.1) | copy-start | bytes 147460
  1.7 0.7 copy-start.2

commit v8 on v7

--- a/solution.py
+++ b/solution.py
@@ -250,6 +250,7 @@
     take_keys(5, 3)
     tiles(x, 5, 3)
     tiles(across, 4, 4)
+
     for i in (1, 3):
         tiles(take_rows(i), 0, 4, 2)
 
@@ -267,7 +268,6 @@
     stat[2] = mixed
     for i in (2, 1, 3):
         send(f"st{i}", stat, stat_in.at[i], on_x(i))
-    dqt[...] = jnp.zeros_like(dqt)
 
     def turn_keys(kc, _):
         kt[kc] = jnp.transpose(kvu[kc].astype(F32))[:HEAD].astype(BF16)
@@ -325,10 +325,9 @@
 
         def rows_step(rt, dkv):
             p = prob[rt, kc] * fac[kc, pl.ds(rt, 1)]
-            ds = (p * (grad[rt, kc] - delta[pl.ds(rt, 1)])).astype(BF16)
-            dkv = dkv + dot(p.astype(BF16), wg[rt]) + dot(ds, wq[rt])
-            dqt[rt] += dot(kt[kc], ds)
-            return dkv
+            ds = p * (grad[rt, kc] - delta[pl.ds(rt, 1)])
+            grad[rt, kc] = ds
+            return dkv + dot(p.astype(BF16), wg[rt]) + dot(ds.astype(BF16), wq[rt])
 
         dkf[...] = lax.fori_loop(0, 8, rows_step, jnp.zeros((RT, WIDE), F32), unroll=8)
         sbs[k] = packed(dkf[pl.ds(pl.multiple_of(128 * (1 - c), 128), 128)]).astype(BF16)
@@ -345,13 +344,15 @@
     lax.fori_loop(0, 8, key_group, 0)
     l1s[6] = both(6).astype(BF16)
     give(6).start()
-    landed(0)
-    for k in (3, 4):
-        landed(k - 2)
-        far = land[0].astype(F32)
-        total = both(k) + land[k - 2].astype(F32)
-        l1s[k] = (total + jnp.where(c == k - 3, far, jnp.zeros_like(far))).astype(BF16)
-        give(k).start()
+
+    def merge():
+        landed(0)
+        for k in (3, 4):
+            landed(k - 2)
+            far = land[0].astype(F32)
+            total = both(k) + land[k - 2].astype(F32)
+            l1s[k] = (total + jnp.where(c == k - 3, far, jnp.zeros_like(far))).astype(BF16)
+            give(k).start()
 
     def row_ways(i, j):
         return pltpu.make_async_remote_copy(
@@ -362,7 +363,14 @@
 
     def rows_out(n, _):
         i = jnp.where(n == 0, 2, jnp.where(n == 1, 1, jnp.where(n == 2, 3, 0)))
-        pair = dqt[pl.ds(((x + i) % 4) * 2, 2)].reshape(WIDE, RT)
+
+        for m in range(2):
+            rt = ((x + i) % 4) * 2 + m
+            part = jnp.zeros((HEAD, RT), F32)
+            for kc in range(8):
+                part = part + dot(kt[kc], grad[rt, kc].astype(BF16))
+            dqt[m] = part
+        pair = dqt[...].reshape(WIDE, RT)
         rows = (jnp.transpose(pair) * SCALE).reshape(4, TOK, WIDE)
         dqb[i] = jnp.concatenate([rows[:, :32], rows[:, 32:]], axis=2).astype(BF16)
         for j in (2, 1, 3):
@@ -370,6 +378,7 @@
         pl.when(i > 0)(row_ways(i, 0).start)
         return 0
 
+    merge()
     lax.fori_loop(0, 4, rows_out, 0)
     dqr[0, y] = dqb[0, 0]
 
@@ -473,7 +482,7 @@
             pltpu.VMEM((4, 3, 8, RT), F32),
             pltpu.VMEM((8, 8, RT), F32),
             pltpu.VMEM((8, RT), F32),
-            pltpu.VMEM((8, HEAD, RT), F32),
+            pltpu.VMEM((2, HEAD, RT), F32),
             pltpu.VMEM((RT, WIDE), F32),
             pltpu.VMEM((8, 2, 32, 2 * WIDE), F32),
             pltpu.VMEM((8, 2, 32, 2 * WIDE), BF16),

time: 69.8 us -> 69.3 us (level)
  no operation moved by 1% of the time
where the time goes in v8:
time: 69.3 us; the launch traced here: 68.9 us
  Pallas kernels  65.1 us (94%)
  local copies, waits for them, and re-layouts  3.1 us (4%)
    pallas_call x1, Pallas kernels, per_device(): pl.pallas_call(kernel, out_shape=[jax.ShapeDtypeStruct((4, TOK, WIDE), BF...  65.1 us
    unnamed x7, local copies, waits for them, and re-layouts  1.4 us

profile of v8, /device:TPU:1, one launch (start us, length us, event | category | flops | bytes accessed | tf_op | source)
XLA Modules:
  0.0 68.9 jit_solution(4618291758702169742)
XLA Ops:
  0.6 0.0 copy-start.1
  0.6 0.0 copy-start
  0.7 1.0 %copy_bitcast_fusion = (bf16[4,64,192]{2,1,0:T(8,128)(2,1)S(1)}, bf16[4,64,192]{2,1,0:T(8,128)(2,1)S(1)}) fusion(bf16[64,4,192]{2,1,0:T(4,128)(2,1)} %param.8, bf16[64,4,192]{2,1,0:T(4,128)(2,1)} %param.5), kind=kLoop, calls=%fused_computation | loop fusion | bytes 393216 | tf_op jit(solution)/shard_map/transpose | solution.py:506
  1.7 0.0 copy-start.2
  1.7 0.0 copy-done.1
  1.7 0.0 copy-done
  1.7 0.6 copy-done.2
  2.3 65.1 %shard_map.76 = (bf16[4,64,192]{2,1,0:T(8,128)(2,1)S(1)}, bf16[64,192]{1,0:T(8,128)(2,1)S(1)}) custom-call(s32[128]{0:T(128)S(1)} %copy-done.2, bf16[4,64,192]{2,1,0:T(8,128)(2,1)S(1)} %get-tuple-element.13.q_in, bf16[4,64,192]{2,1,0:T(8,128)(2,1)S(1)} %get-tuple-element.12.g_in, bf16[64,384]{1,0:T(8,128)(2,1)S(1)} %copy-done, bf16[64,384]{1,0:T(8,128)(2,1)S(1)} %copy-done.1), custom_call_target="tpu_custom_call" | custom-call | tf_op jit(solution)/shard_map/pallas_call | solution.py:459
  67.5 0.8 %copy.10 = bf16[64,4,192]{2,1,0:T(4,128)(2,1)} copy(bf16[64,4,192]{2,0,1:T(8,128)(2,1)S(1)} %bitcast.5) | data formatting | bytes 196608
  68.2 0.7 fusion
Async XLA Ops:
  0.6 1.1 %copy-start.1 = (bf16[64,384]{1,0:T(8,128)(2,1)S(1)}, bf16[64,384]{1,0:T(8,128)(2,1)}, u32[]{:S(2)}) copy-start(bf16[64,384]{1,0:T(8,128)(2,1)} %v_in.1) | copy-start | bytes 147460
  0.6 1.1 %copy-start = (bf16[64,384]{1,0:T(8,128)(2,1)S(1)}, bf16[64,384]{1,0:T(8,128)(2,1)}, u32[]{:S(2)}) copy-start(bf16[64,384]{1,0:T(8,128)(2,1)} %k_in.1) | copy-start | bytes 147460
  1.7 0.7 copy-start.2
